TPU v7x, 32 devices: a whole 2x2x4 slice. The times are simulated.
32 devices in a mesh: section: 4 (over x, core), feat: 8 (over z, y).
Axes of the slice: x: 2, y: 2, z: 4, core: 2. Of those that a mesh axis runs over, the one named last changes fastest.
Arguments:
- residual: bfloat16 [4, 128, 4096], P('section'), may hold values from -6 to 6
- enc_weight: bfloat16 [4, 4096, 16384], P('section', None, 'feat'), may hold values from -0.09375 to 0.09375
- dec_weight: bfloat16 [4, 16384, 4, 4096], P('section', 'feat'), may hold values from -1 to 1
- latent_ids: int32 [4, 128, 64], P('section'), may hold values from 0 to 16383, all different within a row
Outputs:
- written: bfloat16 [4, 4096, 128], P('section', 'feat')
Inputs may be any that keep to these rules, and one draw needn't show every extreme that they name: Each row latent_ids[l, n, :] names 64 different latents.
All inputs are finite; a program needn't handle non-finite values.
Results may differ from a plain program's by a relative error of at most 0.0049.
Values may be sent and summed in bfloat16 or wider, within the bound.
No kernel may reach another device: no remote copies, remote signals or barrier semaphores. Data moves between devices by JAX's collectives and lax.ppermute only.
A program may use at most 192 MiB of HBM per device.

v0:
```python
import jax
import jax.numpy as jnp
from jax import lax
from jax.sharding import PartitionSpec as P


def prefix(shard, axis, combine, identity):
    size, here = (lax.axis_size(axis), lax.axis_index(axis))
    everything = lax.all_gather(shard, axis)
    start = jnp.broadcast_to(jnp.asarray(identity, shard.dtype), shard.shape)

    def hop(k, before):
        reached = k < here
        new = combine(before, everything[k])
        return jnp.where(reached, new, before)

    return lax.fori_loop(0, size, hop, start)


def add_terms(earlier, later):
    return earlier + later


def local(residual, enc_weight, dec_weight, latent_ids):
    section_pos = lax.axis_index("section")
    feat_pos = lax.axis_index("feat")
    layers = lax.axis_size("section")
    shard_size = enc_weight.shape[2]
    pre_acts = jnp.dot(residual[0], enc_weight[0], preferred_element_type=jnp.float32)
    local_ids = latent_ids[0] - feat_pos * shard_size
    lane_ids = lax.broadcasted_iota(jnp.int32, (1, 1, shard_size), 2)
    active = jnp.sum((local_ids[:, :, None] == lane_ids).astype(jnp.float32), axis=1)
    latent_acts = (jnp.maximum(pre_acts, 0.0) * active).astype(jnp.bfloat16)
    weights = dec_weight[0]
    targets = lax.broadcasted_iota(jnp.int32, (layers,), 0)
    keep_mask = (targets >= section_pos).astype(jnp.float32)
    summed = lax.psum_scatter(
        jnp.einsum("nf,flc->cln", latent_acts, weights, preferred_element_type=jnp.float32),
        "feat",
        scatter_dimension=0,
        tiled=True,
    )
    partial_value = jnp.transpose(summed, (1, 0, 2))
    partial_value = partial_value * keep_mask[:, None, None]
    before = prefix(partial_value, "section", add_terms, jnp.zeros_like(partial_value))
    own_block = lax.dynamic_index_in_dim(before + partial_value, section_pos, 0, keepdims=True)
    written = own_block.astype(jnp.bfloat16)
    return written


def solution(mesh):
    in_specs = (
        P("section", None, None),
        P("section", None, "feat"),
        P("section", "feat", None, None),
        P("section", None, None),
    )
    out_specs = P("section", "feat", None)
    return jax.shard_map(local, mesh=mesh, in_specs=in_specs, out_specs=out_specs, check_vma=False)
```

profile of v0, /device:TPU:0, one launch (start us, length us, event | category | flops | bytes accessed | tf_op | source)
XLA Modules:
  0.0 349.4 jit_solution(17416771416902703555)
XLA Ops:
  6.5 0.0 copy-start
  6.5 0.0 reduce-scatter.2.cloned.1.call-start
  6.5 0.8 subtract_bitcast_fusion
  7.4 0.1 copy.15
  7.5 11.4 %convert_reduce_fusion = f32[128,2048]{1,0:T(8,128)S(1)} fusion(s32[128,64]{1,0:T(8,128)S(1)} %copy.15), kind=kLoop, calls=%fused_computation.3 | loop fusion | flops 50069504 | bytes 1081344 | tf_op jit(solution)/shard_map/reduce_sum | solution.py:32
  18.9 0.0 copy-done
  18.9 8.2 %fusion.16 = bf16[128,2048,1]{1,0,2:T(8,128)(2,1)S(1)} fusion(f32[128,2048]{1,0:T(8,128)S(1)} %convert_reduce_fusion, bf16[1,4096,2048]{2,1,0:T(8,128)(2,1)} %param.7, bf16[1,128,4096]{2,1,0:T(8,128)(2,1)S(1)} %copy-done), kind=kOutput, calls=%fused_computation.11 | convolution fusion | flops 2148270080 | bytes 19398656 | tf_op jit(solution)/shard_map/dot_general | solution.py:29
  27.1 117.4 %fusion.4 = f32[4096,4,128]{0,2,1:T(8,128)} fusion(bf16[128,2048,1]{1,0,2:T(8,128)(2,1)S(1)} %fusion.16, bf16[2048,4,4096]{2,1,0:T(4,128)(2,1)} %bitcast.4), kind=kOutput, calls=%fused_computation.7 | convolution fusion | flops 8589934592 | bytes 76021760 | tf_op jit(solution)/shard_map/nf,flc->cln/dot_general | solution.py:38
  144.5 0.0 reduce-scatter.2.cloned.1.call-update
  144.5 0.0 all-gather.3.cloned.1.call-start
  144.5 152.2 %reduce-scatter.2.cloned.1.call-done = f32[512,4,128]{0,2,1:T(8,128)} async-done(((f32[4096,4,128]{0,2,1:T(8,128)}), f32[512,4,128]{0,2,1:T(8,128)}) %reduce-scatter.2.cloned.1.call-update) | async-done | bytes 1048592 | tf_op jit(solution)/shard_map/reduce_scatter | solution.py:37
  296.7 1.4 multiply_bitcast_fusion
  298.2 1.3 copy.17
  299.5 0.0 all-gather.3.cloned.1.call-update
  299.5 33.6 %all-gather.3.cloned.1.call-done = f32[16,512,128]{2,1,0:T(8,128)} async-done(((f32[4,512,128]{2,1,0:T(8,128)}), f32[16,512,128]{2,1,0:T(8,128)}) %all-gather.3.cloned.1.call-update) | async-done | bytes 4194320 | tf_op jit(solution)/shard_map/all_gather | solution.py:9
  333.2 6.3 %while.14 = (s32[]{:T(128)}, f32[4,512,128]{2,1,0:T(8,128)S(1)}, s32[]{:T(128)}, f32[4,4,512,128]{3,2,1,0:T(8,128)}, s32[]{:T(128)}, /*index=5*/s32[]{:T(128)}) while((s32[]{:T(128)}, f32[4,512,128]{2,1,0:T(8,128)S(1)}, s32[]{:T(128)}, f32[4,4,512,128]{3,2,1,0:T(8,128)}, s32[]{:T(128)}, /*index=5*/s32[]{:T(128)}) %tuple.40), condition=%wide.region_3.4_spmd.clone, body=%wide.region_2.3_spmd.clone.sunk | while | flops 786436 | bytes 3145829 | solution.py:17
  333.2 1.6 add_select_fusion.2
  334.7 1.6 add_select_fusion.2
  336.3 1.6 add_select_fusion.2
  337.9 1.6 add_select_fusion.2
  339.5 1.3 copy.18
  340.8 1.0 fusion.20
  341.8 0.8 copy.19
  (2 shorter events, 0.0 us)
Async XLA Ops:
  6.5 12.4 %copy-start = (bf16[1,128,4096]{2,1,0:T(8,128)(2,1)S(1)}, bf16[1,128,4096]{2,1,0:T(8,128)(2,1)}, u32[]{:S(2)}) copy-start(bf16[1,128,4096]{2,1,0:T(8,128)(2,1)} %param.6) | copy-start | bytes 3145732
  6.5 290.2 %reduce-scatter.2.cloned.1.call-start = ((), (), s32[]{:S(2)}) async-start(), calls=%async_computation.1 | async-start | bytes 9437184 | tf_op jit(solution)/shard_map/reduce_scatter | solution.py:37
  144.5 188.7 %all-gather.3.cloned.1.call-start = ((), (), s32[]{:S(2)}) async-start(), calls=%async_computation.2 | async-start | bytes 5242880 | tf_op jit(solution)/shard_map/all_gather | solution.py:9
Sparse Core Ops, SparseCore 0:
  144.6 152.0 reduce-scatter.1
  299.6 33.4 all-gather.2
where the time goes:
time: 350 us; the launch traced here: 349 us
  waiting for transfers between devices  186 us (53%)
  matrix products  126 us (36%)
  other arithmetic  20.9 us (6%)
  between operations  13.5 us (4%)
    reduce_scatter x1, waiting for transfers between devices, local(): lax.psum_scatter(jnp.einsum('nf,flc->cln', latent_acts, weights, preferre...  152 us
    dot_general x1, matrix products, local(): jnp.einsum('nf,flc->cln', latent_acts, weights, preferred_element_type=jn...  117 us
    all_gather x1, waiting for transfers between devices, prefix(): everything = lax.all_gather(shard, axis)  33.6 us
    reduce_sum x1, other arithmetic, local(): jnp.sum((local_ids[:, :, None] == lane_ids).astype(jnp.float32), axis=1)  11.4 us
    dot_general x1, matrix products, local(): jnp.dot(residual[0], enc_weight[0], preferred_element_type=jnp.float32)  8.17 us
  transfers between devices with their start and end apart: 2, of which 2 were waited for; matrix products, arithmetic and copies ran while one was open for 0% of the time, Pallas kernels for 0%

commit v1 on v0

v1 whole, which is shorter than its diff:
```python
import functools

import jax
import jax.numpy as jnp
from jax import lax
from jax.experimental import pallas as pl
from jax.experimental.pallas import tpu as pltpu
from jax.sharding import PartitionSpec as P

LANES = 128
GROUP = 4
RING = 2
WIDE = 4
ENC_SLOTS = 4
F32 = jnp.float32
BF16 = jnp.bfloat16


def iota(shape, dim):
    return lax.broadcasted_iota(jnp.int32, shape, dim)


def dot(a, b):
    return jnp.dot(a, b, preferred_element_type=F32)


def dot_t(a, b):
    return lax.dot_general(a, b, (((1,), (1,)), ((), ())), preferred_element_type=F32)


def kernel(
    feats,
    relative,
    pos_ref,
    ids_hbm,
    res_hbm,
    enc_hbm,
    dec_hbm,
    out_hbm,
    ids_v,
    lo_v,
    sh_v,
    res_v,
    enc_v,
    list_v,
    list_s,
    pre_v,
    acts_v,
    lhs_v,
    buf,
    acc,
    out_v,
    small_sem,
    enc_sem,
    dec_sem,
    out_sem,
):
    tokens, width = res_v.shape
    shard = acts_v.shape[1]
    slots = list_v.shape[1]
    rows_hi = shard // LANES
    max_blocks = slots // LANES
    wides = out_v.shape[1]
    section_pos, feat_pos = pos_ref[0], pos_ref[1]
    core = section_pos % 2

    ids_copy = pltpu.make_async_copy(ids_hbm, ids_v, small_sem.at[0])
    ids_copy.start()
    res_copy = pltpu.make_async_copy(res_hbm, res_v, small_sem.at[1])
    res_copy.start()
    depth = enc_v.shape[1]
    enc_steps = width // depth

    def enc_copy(step):
        return pltpu.make_async_copy(
            enc_hbm.at[pl.ds(step * depth, depth)], enc_v.at[step % ENC_SLOTS], enc_sem.at[step % ENC_SLOTS]
        )

    for step in range(min(ENC_SLOTS, enc_steps)):
        enc_copy(step).start()

    ids_copy.wait()
    local = ids_v[...] - feat_pos * shard
    inside = (local >= 0) & (local < shard)
    lo_v[...] = jnp.where(inside, local & (LANES - 1), -1)
    sh_v[...] = jnp.where(inside, jnp.left_shift(1, (local >> 7) & 31), 0)
    lane_of = iota((LANES, tokens), 0)

    def gather_bits(k, bits):
        hit = lo_v[pl.ds(k, 1), :] == lane_of
        return bits | jnp.where(hit, sh_v[pl.ds(k, 1), :], 0)

    bits_t = lax.fori_loop(0, ids_v.shape[0], gather_bits, jnp.zeros((LANES, tokens), jnp.int32), unroll=8)
    bits = bits_t.T
    union = bits
    while union.shape[0] > 1:
        half = union.shape[0] // 2
        union = union[:half] | union[half:]

    hi_of = iota((LANES, LANES), 0)
    lane = iota((LANES, LANES), 1)
    flags = jnp.where(hi_of < rows_hi, jnp.right_shift(jnp.broadcast_to(union, (LANES, LANES)), hi_of & 31) & 1, 0)
    flags_f = flags.astype(F32)
    flags_b = flags_f.astype(BF16)
    upper = (hi_of <= lane).astype(F32).astype(BF16)
    inclusive = dot(flags_b, upper)
    row_total = jnp.sum(flags_f, axis=1, keepdims=True)
    below = (lane < hi_of).astype(F32).astype(BF16)
    row_start = dot(below, jnp.broadcast_to(row_total, (LANES, LANES)).astype(BF16))
    row_end = row_start + row_total
    count = jnp.sum(flags_f).astype(jnp.int32)
    rank = jnp.where(flags > 0, row_start + inclusive - 1.0, -1.0)

    slot = iota((LANES, slots), 1).astype(F32)
    start_w = jnp.concatenate([row_start] * max_blocks, axis=1)
    end_w = jnp.concatenate([row_end] * max_blocks, axis=1)
    in_row = (start_w <= slot) & (slot < end_w)
    in_row_f = in_row.astype(F32)
    row_of = jnp.sum(in_row_f * iota((LANES, slots), 0).astype(F32), axis=0, keepdims=True)
    place = jnp.sum(jnp.where(in_row, slot - start_w, 0.0), axis=0, keepdims=True)
    prefix = dot(inclusive.T.astype(BF16), in_row_f.astype(BF16))
    lane_in = jnp.sum((prefix <= place).astype(F32), axis=0, keepdims=True)
    latent = row_of * float(LANES) + lane_in
    latent = jnp.where(iota((1, slots), 1) < count, latent, 0.0).astype(jnp.int32)
    list_v[...] = latent
    list_copy = pltpu.make_async_copy(list_v, list_s, small_sem.at[2])
    list_copy.start()
    blocks = jnp.maximum(1, (count + (LANES - 1)) // LANES)
    groups = (blocks + (GROUP - 1)) // GROUP

    def issue(group):
        ring = lax.rem(group, RING)
        here = jnp.minimum(GROUP, blocks - group * GROUP)

        def block(b, carry):
            place = ring * GROUP + b
            base = (group * GROUP + b) * LANES

            def row(i, carry):
                latent_id = list_s[0, base + i]
                pltpu.make_async_copy(
                    dec_hbm.at[latent_id],
                    buf.at[place, :, :, pl.ds(pl.multiple_of(2 * i, 2), 2), :],
                    dec_sem.at[place],
                ).start()
                return carry

            return lax.fori_loop(0, LANES, row, carry, unroll=8)

        lax.fori_loop(0, here, block, 0)

    def encode(step):
        enc_copy(step).wait()
        part = dot(res_v[:, pl.ds(step * depth, depth)], enc_v[step % ENC_SLOTS])
        if step == 0:
            pre_v[...] = part
        else:
            pre_v[...] += part
        if step + ENC_SLOTS < enc_steps:
            enc_copy(step + ENC_SLOTS).start()

    res_copy.wait()
    early = min(2, enc_steps)
    for step in range(early):
        encode(step)
    list_copy.wait()
    issue(0)
    for step in range(early, enc_steps):
        encode(step)

    for hi in range(rows_hi):
        columns = slice(hi * LANES, (hi + 1) * LANES)
        active = (jnp.right_shift(bits, hi) & 1) > 0
        acts_v[:, columns] = jnp.where(active, jnp.maximum(pre_v[:, columns], 0.0), 0.0).astype(BF16)

    @pl.when(groups > 1)
    def _():
        issue(1)

    twice = ((iota((LANES, 2 * LANES), 1) >> 1) == iota((LANES, 2 * LANES), 0)).astype(F32).astype(BF16)
    parity = iota((tokens, 2 * LANES), 1) & 1

    def compact(b, carry):
        want = (iota((LANES, LANES), 0) + b * LANES).astype(F32)
        chosen = jnp.concatenate(
            [(rank[hi : hi + 1, :] == want).astype(F32).astype(BF16) for hi in range(rows_hi)], axis=1
        )
        picked = dot_t(acts_v[...], chosen).astype(BF16)
        doubled = dot(picked, twice)
        lhs_v[b, :tokens, :] = jnp.where(parity == core, doubled, 0.0).astype(BF16)
        lhs_v[b, tokens:, :] = jnp.where(parity == core, 0.0, doubled).astype(BF16)
        return carry

    lax.fori_loop(0, blocks, compact, 0)

    def out_copy(pair, wide, dest):
        return pltpu.make_async_copy(out_v.at[pair, wide], out_hbm.at[:, pair, dest], out_sem)

    def multiply(group, size, first, last):
        ring = lax.rem(group, RING)
        for b in range(size):
            place = ring * GROUP + b
            pltpu.make_async_copy(buf.at[place], buf.at[place], dec_sem.at[place]).wait()
        left = jnp.concatenate([lhs_v[group * GROUP + b] for b in range(size)], axis=1)

        def wide_step(i, carry):
            pair = i // wides
            wide = lax.rem(i, wides)
            right = jnp.concatenate(
                [
                    jnp.concatenate([buf[ring * GROUP + b, wide * WIDE + q, pair] for q in range(WIDE)], axis=1)
                    for b in range(size)
                ],
                axis=0,
            )
            total = dot(left, right)
            if not first:
                total = total + acc[pair, wide]
            if last:
                narrow = total.astype(BF16)
                for part in range(2):
                    for q in range(WIDE):
                        out_v[pair, wide, part, q] = narrow[
                            part * tokens : (part + 1) * tokens, q * LANES : (q + 1) * LANES
                        ]
                if relative:
                    apart = jnp.bitwise_xor(wide, feat_pos)
                    dest = (apart & 1) * (feats // 2) + (apart >> 1)
                else:
                    dest = wide
                out_copy(pair, wide, dest).start()
            else:
                acc[pair, wide] = total
            return carry

        lax.fori_loop(0, 2 * wides, wide_step, 0)

    def each_group(group, carry):
        here = blocks - group * GROUP
        for first in (True, False):
            at = (group == 0) if first else (group > 0)
            if max_blocks > GROUP:

                @pl.when(at & (here > GROUP))
                def _():
                    multiply(group, GROUP, first, False)

            elif not first:
                continue
            for size in range(1, min(GROUP, max_blocks) + 1):

                @pl.when(at & (here == size))
                def _():
                    multiply(group, size, first, True)

        if max_blocks > RING * GROUP:

            @pl.when(group + RING < groups)
            def _():
                issue(group + RING)

        return carry

    lax.fori_loop(0, groups, each_group, 0)
    for pair in range(2):
        for wide in range(wides):
            out_copy(pair, wide, 0).wait()


def partial_sums(position, ids, residual, enc, dec, feats, relative):
    tokens, width = residual.shape
    shard = enc.shape[1]
    tiles = width // LANES
    wides = tiles // WIDE
    max_blocks = -(-shard // LANES)
    slots = max_blocks * LANES
    depth = min(512, width)
    return pl.pallas_call(
        functools.partial(kernel, feats, relative),
        out_shape=jax.ShapeDtypeStruct((2, 2, wides, WIDE, tokens, LANES), BF16),
        in_specs=[pl.BlockSpec(memory_space=pltpu.SMEM)] + [pl.BlockSpec(memory_space=pl.ANY)] * 4,
        out_specs=pl.BlockSpec(memory_space=pl.ANY),
        scratch_shapes=[
            pltpu.VMEM(ids.shape, jnp.int32),
            pltpu.VMEM(ids.shape, jnp.int32),
            pltpu.VMEM(ids.shape, jnp.int32),
            pltpu.VMEM((tokens, width), BF16),
            pltpu.VMEM((ENC_SLOTS, depth, shard), BF16),
            pltpu.VMEM((1, slots), jnp.int32),
            pltpu.SMEM((1, slots), jnp.int32),
            pltpu.VMEM((tokens, shard), F32),
            pltpu.VMEM((tokens, shard), BF16),
            pltpu.VMEM((max_blocks, 2 * tokens, 2 * LANES), BF16),
            pltpu.VMEM((min(RING * GROUP, max_blocks), tiles, 2, 2 * LANES, LANES), BF16),
            pltpu.VMEM((2, wides, 2 * tokens, WIDE * LANES), F32),
            pltpu.VMEM((2, wides, 2, WIDE, tokens, LANES), BF16),
            pltpu.SemaphoreType.DMA((3,)),
            pltpu.SemaphoreType.DMA((ENC_SLOTS,)),
            pltpu.SemaphoreType.DMA((RING * GROUP,)),
            pltpu.SemaphoreType.DMA,
        ],
        compiler_params=pltpu.CompilerParams(vmem_limit_bytes=62 * 2**20),
        cost_estimate=pl.CostEstimate(
            flops=4 * tokens * width * shard, bytes_accessed=2 * width * shard * 3, transcendentals=0
        ),
    )(position, ids, residual, enc, dec)


def local(residual, enc_weight, dec_weight, latent_ids):
    feats = lax.axis_size("feat")
    section_pos = lax.axis_index("section")
    feat_pos = lax.axis_index("feat")
    tokens, width = residual.shape[1:]
    shard = enc_weight.shape[2]
    tiles = width // LANES
    own = width // feats
    relative = own == WIDE * LANES
    position = jnp.stack([section_pos, feat_pos]).astype(jnp.int32)
    ids = latent_ids[0].T
    dec = dec_weight[0].reshape(shard, 2, 2, tiles, LANES).transpose(0, 3, 1, 2, 4)
    sums = partial_sums(position, ids, residual[0], enc_weight[0], dec, feats, relative)
    if relative:
        blocks = sums.reshape(2, 2, 2, feats // 2, WIDE, tokens, LANES)
    else:
        blocks = jnp.transpose(sums, (0, 1, 2, 3, 5, 4)).reshape(2, 2, feats, own, tokens)
        apart = jnp.arange(feats)
        apart = (apart % (feats // 2)) * 2 + apart // (feats // 2)
        blocks = jnp.take(blocks, apart ^ feat_pos, axis=2).reshape(2, 2, 2, feats // 2, own, tokens)
    keep, send = blocks[0], blocks[1]

    def across_feat(x, bit, sections):
        pairs = [(s * feats + f, s * feats + (f ^ bit)) for s in sections for f in range(feats)]
        return lax.ppermute(x, ("section", "feat"), pairs)

    def reduce_feat(x, sections):
        x = x.astype(F32)
        half = x[0] + across_feat(x[1].astype(BF16), 1, sections).astype(F32)
        narrow = half.astype(BF16)
        total = half[0]
        for device in range(1, feats // 2):
            total = total + across_feat(narrow[device], 2 * device, sections).astype(F32)
        return total

    late = keep[1].astype(F32) + lax.ppermute(send[1], "section", [(0, 1), (1, 0), (2, 3)]).astype(F32)
    early = keep[0].astype(F32) + lax.ppermute(send[0], "section", [(0, 1)]).astype(F32)
    late = reduce_feat(late, (0, 1, 2, 3))
    early = reduce_feat(early, (0, 1))
    carried = lax.ppermute(late, "section", [(0, 2), (1, 3)])
    written = jnp.where(section_pos < 2, early, late + carried)
    if relative:
        written = jnp.transpose(written, (0, 2, 1)).reshape(own, tokens)
    return written.astype(BF16)[None]


def solution(mesh):
    in_specs = (
        P("section", None, None),
        P("section", None, "feat"),
        P("section", "feat", None, None),
        P("section", None, None),
    )
    out_specs = P("section", "feat", None)
    return jax.shard_map(local, mesh=mesh, in_specs=in_specs, out_specs=out_specs, check_vma=False)
```

time: 350 us -> 94.5 us (0.27)
  waiting for transfers between devices: 186 us -> 27.5 us
  matrix products: 126 us -> 0 us
  Pallas kernels: 0 us -> 32.8 us
  starting transfers between devices: 0.04 us -> 28.1 us
  other arithmetic: 20.9 us -> 1.89 us
  between operations: 13.5 us -> 0.17 us
    reduce_scatter x1 -> x0, waiting for transfers between devices: 152 us -> none  [local(): lax.psum_scatter(jnp.einsum('nf,flc->cln', latent_acts, weights, preferre...]
    dot_general x2 -> x0, matrix products: 126 us -> none  [the longest x1 117 us: local(): jnp.einsum('nf,flc->cln', latent_acts, weights, preferred_element_type=jn...]
    all_gather x1 -> x0, waiting for transfers between devices: 33.6 us -> none  [prefix(): everything = lax.all_gather(shard, axis)]
    pallas_call x0 -> x1, Pallas kernels: none -> 32.8 us  [partial_sums(): pl.pallas_call(functools.partial(kernel, feats, relative), out_shape=jax....]
    ppermute x0 -> x11, starting transfers between devices: none -> 28.1 us  [the longest x8 20.4 us: across_feat(): return lax.ppermute(x, ('section', 'feat'), pairs)]
    ppermute x0 -> x11, waiting for transfers between devices: none -> 27.5 us  [the longest x8 27.2 us: across_feat(): return lax.ppermute(x, ('section', 'feat'), pairs)]
    reduce_sum x1 -> x0, other arithmetic: 11.4 us -> none  [local(): jnp.sum((local_ids[:, :, None] == lane_ids).astype(jnp.float32), axis=1)]
    select_n x4 -> x0, other arithmetic: 6.27 us -> none  [hop(): return jnp.where(reached, new, before)]
  transfers between devices with their start and end apart: 2 -> 11, of which waited for: 2 -> 7; matrix products, arithmetic and copies ran while one was open for 0% -> 1% of each run, Pallas kernels for 0% -> 0%
where the time goes in v1:
time: 94.5 us; the launch traced here: 94.2 us
  Pallas kernels  32.8 us (35%)
  starting transfers between devices  28.1 us (30%)
  waiting for transfers between devices  27.5 us (29%)
  local copies, waits for them, and re-layouts  3.76 us (4%)
  other arithmetic  1.89 us (2%)
    pallas_call x1, Pallas kernels, partial_sums(): pl.pallas_call(functools.partial(kernel, feats, relative), out_shape=jax....  32.8 us
    ppermute x8, waiting for transfers between devices, across_feat(): return lax.ppermute(x, ('section', 'feat'), pairs)  27.2 us
    ppermute x8, starting transfers between devices, across_feat(): return lax.ppermute(x, ('section', 'feat'), pairs)  20.4 us
    ppermute x1, starting transfers between devices, local(): carried = lax.ppermute(late, 'section', [(0, 2), (1, 3)])  3.36 us
    slice x1, local copies, waits for them, and re-layouts, local(): send[0]  2.75 us
    ppermute x1, starting transfers between devices, local(): lax.ppermute(send[1], 'section', [(0, 1), (1, 0), (2, 3)]).astype(F32)  2.37 us
    ppermute x1, starting transfers between devices, local(): lax.ppermute(send[0], 'section', [(0, 1)]).astype(F32)  2.02 us
  transfers between devices with their start and end apart: 11, of which 7 were waited for; matrix products, arithmetic and copies ran while one was open for 1% of the time, Pallas kernels for 0%

profile of v1, /device:TPU:0, one launch (start us, length us, event | category | flops | bytes accessed | tf_op | source)
XLA Modules:
  0.0 94.2 jit_solution(6828017424257266145)
XLA Ops:
  0.0 0.7 pad_add_fusion.pos_ref
  0.7 32.8 %shard_map.46 = bf16[2,2,8,4,128,128]{5,4,3,2,1,0:T(8,128)(2,1)} custom-call(s32[2]{0:T(128)} %pad_add_fusion.pos_ref, s32[64,128]{1,0:T(8,128)} %bitcast.73, bf16[128,4096]{1,0:T(8,128)(2,1)} %bitcast.70, bf16[4096,2048]{1,0:T(8,128)(2,1)} %bitcast.67, bf16[2048,32,2,2,128]{4,3,2,1,0:T(2,128)(2,1)} %bitcast.7.dec_hbm), custom_call_target="tpu_custom_call" | custom-call | flops 4294967296 | bytes 50331648 | tf_op jit(solution)/shard_map/pallas_call | solution.py:278
  33.5 2.8 %fusion.17 = (bf16[1,1,8,4,128,128]{5,4,3,2,1,0:T(8,128)(2,1)S(1)}, bf16[1,1,8,4,128,128]{5,4,3,2,1,0:T(8,128)(2,1)S(1)}, bf16[1,1,8,4,128,128]{5,4,3,2,1,0:T(8,128)(2,1)S(1)}, bf16[1,1,8,4,128,128]{5,4,3,2,1,0:T(8,128)(2,1)S(1)}) fusion(bf16[2,2,8,4,128,128]{5,4,3,2,1,0:T(8,128)(2,1)} %shard_map.46), kind=kLoop, calls=%fused_computation.30 | loop fusion | bytes 8388608 | tf_op jit(solution)/shard_map/slice | solution.py:345
  36.2 2.4 %collective-permute-start.5 = (bf16[2,4,4,128,128]{4,3,2,1,0:T(8,128)(2,1)S(1)}, bf16[2,4,4,128,128]{4,3,2,1,0:T(8,128)(2,1)S(1)}, u32[]{:S(2)}, u32[]{:S(2)}) collective-permute-start(bf16[2,4,4,128,128]{4,3,2,1,0:T(8,128)(2,1)S(1)} %bitcast.72), channel_id=1, source_target_pairs={{0,8},{8,0},{16,24},{1,9},{9,1},{17,25},{2,10},{10,2},{18,26},{3,1... | collective-permute-start | bytes 3145736 | tf_op jit(solution)/shard_map/ppermute | solution.py:344
  38.6 2.0 %collective-permute-start = (bf16[2,4,4,128,128]{4,3,2,1,0:T(8,128)(2,1)S(1)}, bf16[2,4,4,128,128]{4,3,2,1,0:T(8,128)(2,1)S(1)}, u32[]{:S(2)}, u32[]{:S(2)}) collective-permute-start(bf16[2,4,4,128,128]{4,3,2,1,0:T(8,128)(2,1)S(1)} %bitcast.71), channel_id=1, source_target_pairs={{0,8},{1,9},{2,10},{3,11},{4,12},{5,13},{6,14},{7,15}} | collective-permute-start | bytes 3145736 | tf_op jit(solution)/shard_map/ppermute | solution.py:345
  40.6 0.2 collective-permute-done.5
  40.9 0.3 convert_add_fusion
  41.2 0.1 fusion.3
  41.3 2.9 %collective-permute-start.6 = (bf16[4,4,128,128]{3,2,1,0:T(8,128)(2,1)S(1)}, bf16[4,4,128,128]{3,2,1,0:T(8,128)(2,1)S(1)}, u32[]{:S(2)}, u32[]{:S(2)}) collective-permute-start(bf16[4,4,128,128]{3,2,1,0:T(8,128)(2,1)S(1)} %fusion.3), channel_id=1, source_target_pairs={{0,1},{1,0},{2,3},{3,2},{4,5},{5,4},{6,7},{7,6},{8,9},{9,8},{10,11... | collective-permute-start | bytes 1572872 | tf_op jit(solution)/shard_map/ppermute | solution.py:333
  44.2 0.0 collective-permute-done
  44.2 0.3 convert_add_fusion.1
  44.6 0.1 fusion.2
  44.7 3.5 %collective-permute-start.1 = (bf16[4,4,128,128]{3,2,1,0:T(8,128)(2,1)S(1)}, bf16[4,4,128,128]{3,2,1,0:T(8,128)(2,1)S(1)}, u32[]{:S(2)}, u32[]{:S(2)}) collective-permute-start(bf16[4,4,128,128]{3,2,1,0:T(8,128)(2,1)S(1)} %fusion.2), channel_id=1, source_target_pairs={{0,1},{1,0},{2,3},{3,2},{4,5},{5,4},{6,7},{7,6},{8,9},{9,8},{10,11... | collective-permute-start | bytes 1572872 | tf_op jit(solution)/shard_map/ppermute | solution.py:333
  48.2 8.8 %collective-permute-done.6 = bf16[4,4,128,128]{3,2,1,0:T(8,128)(2,1)S(1)} collective-permute-done((bf16[4,4,128,128]{3,2,1,0:T(8,128)(2,1)S(1)}, bf16[4,4,128,128]{3,2,1,0:T(8,128)(2,1)S(1)}, u32[]{:S(2)}, u32[]{:S(2)}) %collective-permute-start.6) | collective-permute-done | bytes 524320 | tf_op jit(solution)/shard_map/ppermute | solution.py:333
  56.9 0.2 fusion.15
  57.2 2.2 %collective-permute-start.7 = (bf16[4,128,128]{2,1,0:T(8,128)(2,1)S(1)}, bf16[4,128,128]{2,1,0:T(8,128)(2,1)S(1)}, u32[]{:S(2)}, u32[]{:S(2)}) collective-permute-start(bf16[4,128,128]{2,1,0:T(8,128)(2,1)S(1)} %get-tuple-element.16), channel_id=1, source_target_pairs={{0,2},{1,3},{2,0},{3,1},{4,6},{5,7},{6,4},{7,5},{8,10},{9,11},{10,... | collective-permute-start | bytes 393224 | tf_op jit(solution)/shard_map/ppermute | solution.py:333
  59.3 2.5 %collective-permute-start.9 = (bf16[4,128,128]{2,1,0:T(8,128)(2,1)S(1)}, bf16[4,128,128]{2,1,0:T(8,128)(2,1)S(1)}, u32[]{:S(2)}, u32[]{:S(2)}) collective-permute-start(bf16[4,128,128]{2,1,0:T(8,128)(2,1)S(1)} %get-tuple-element.17), channel_id=1, source_target_pairs={{0,6},{1,7},{2,4},{3,5},{4,2},{5,3},{6,0},{7,1},{8,14},{9,15},{10,... | collective-permute-start | bytes 393224 | tf_op jit(solution)/shard_map/ppermute | solution.py:333
  61.9 0.1 collective-permute-start.8
  62.0 5.7 %collective-permute-done.1 = bf16[4,4,128,128]{3,2,1,0:T(8,128)(2,1)S(1)} collective-permute-done((bf16[4,4,128,128]{3,2,1,0:T(8,128)(2,1)S(1)}, bf16[4,4,128,128]{3,2,1,0:T(8,128)(2,1)S(1)}, u32[]{:S(2)}, u32[]{:S(2)}) %collective-permute-start.1) | collective-permute-done | bytes 524320 | tf_op jit(solution)/shard_map/ppermute | solution.py:333
  67.7 0.2 fusion.13
  67.9 0.0 collective-permute-done.7
  67.9 0.1 collective-permute-done.9
  68.0 4.3 %collective-permute-done.8 = bf16[4,128,128]{2,1,0:T(8,128)(2,1)S(1)} collective-permute-done((bf16[4,128,128]{2,1,0:T(8,128)(2,1)S(1)}, bf16[4,128,128]{2,1,0:T(8,128)(2,1)S(1)}, u32[]{:S(2)}, u32[]{:S(2)}) %collective-permute-start.8) | collective-permute-done | bytes 131104 | tf_op jit(solution)/shard_map/ppermute | solution.py:333
  72.3 0.1 fusion.6
  72.3 3.4 %collective-permute-start.10 = (f32[4,128,128]{2,1,0:T(8,128)S(1)}, f32[4,128,128]{2,1,0:T(8,128)S(1)}, u32[]{:S(2)}, u32[]{:S(2)}) collective-permute-start(f32[4,128,128]{2,1,0:T(8,128)S(1)} %fusion.6), channel_id=1, source_target_pairs={{0,16},{8,24},{1,17},{9,25},{2,18},{10,26},{3,19},{11,27},{4,20},{... | collective-permute-start | bytes 786440 | tf_op jit(solution)/shard_map/ppermute | solution.py:348
  75.7 1.9 %collective-permute-start.2 = (bf16[4,128,128]{2,1,0:T(8,128)(2,1)S(1)}, bf16[4,128,128]{2,1,0:T(8,128)(2,1)S(1)}, u32[]{:S(2)}, u32[]{:S(2)}) collective-permute-start(bf16[4,128,128]{2,1,0:T(8,128)(2,1)S(1)} %get-tuple-element.13), channel_id=1, source_target_pairs={{0,2},{1,3},{2,0},{3,1},{4,6},{5,7},{6,4},{7,5},{8,10},{9,11},{10,... | collective-permute-start | bytes 393224 | tf_op jit(solution)/shard_map/ppermute | solution.py:333
  77.7 4.6 %collective-permute-start.4 = (bf16[4,128,128]{2,1,0:T(8,128)(2,1)S(1)}, bf16[4,128,128]{2,1,0:T(8,128)(2,1)S(1)}, u32[]{:S(2)}, u32[]{:S(2)}) collective-permute-start(bf16[4,128,128]{2,1,0:T(8,128)(2,1)S(1)} %get-tuple-element.14), channel_id=1, source_target_pairs={{0,6},{1,7},{2,4},{3,5},{4,2},{5,3},{6,0},{7,1},{8,14},{9,15},{10,... | collective-permute-start | bytes 393224 | tf_op jit(solution)/shard_map/ppermute | solution.py:333
  82.2 2.7 %collective-permute-start.3 = (bf16[4,128,128]{2,1,0:T(8,128)(2,1)S(1)}, bf16[4,128,128]{2,1,0:T(8,128)(2,1)S(1)}, u32[]{:S(2)}, u32[]{:S(2)}) collective-permute-start(bf16[4,128,128]{2,1,0:T(8,128)(2,1)S(1)} %get-tuple-element.15), channel_id=1, source_target_pairs={{0,4},{1,5},{2,6},{3,7},{4,0},{5,1},{6,2},{7,3},{8,12},{9,13},{10,... | collective-permute-start | bytes 393224 | tf_op jit(solution)/shard_map/ppermute | solution.py:333
  85.0 1.6 %collective-permute-done.4 = bf16[4,128,128]{2,1,0:T(8,128)(2,1)S(1)} collective-permute-done((bf16[4,128,128]{2,1,0:T(8,128)(2,1)S(1)}, bf16[4,128,128]{2,1,0:T(8,128)(2,1)S(1)}, u32[]{:S(2)}, u32[]{:S(2)}) %collective-permute-start.4) | collective-permute-done | bytes 131104 | tf_op jit(solution)/shard_map/ppermute | solution.py:333
  86.5 6.8 %collective-permute-done.3 = bf16[4,128,128]{2,1,0:T(8,128)(2,1)S(1)} collective-permute-done((bf16[4,128,128]{2,1,0:T(8,128)(2,1)S(1)}, bf16[4,128,128]{2,1,0:T(8,128)(2,1)S(1)}, u32[]{:S(2)}, u32[]{:S(2)}) %collective-permute-start.3) | collective-permute-done | bytes 131104 | tf_op jit(solution)/shard_map/ppermute | solution.py:333
  93.3 0.1 fusion.12
  93.4 0.8 copy.5
  (4 shorter events, 0.1 us)
Async XLA Ops:
  36.2 4.6 %collective-permute-start.5 = (bf16[2,4,4,128,128]{4,3,2,1,0:T(8,128)(2,1)S(1)}, bf16[2,4,4,128,128]{4,3,2,1,0:T(8,128)(2,1)S(1)}, u32[]{:S(2)}, u32[]{:S(2)}) collective-permute-start(bf16[2,4,4,128,128]{4,3,2,1,0:T(8,128)(2,1)S(1)} %bitcast.72), channel_id=1, source_target_pairs={{0,8},{8,0},{16,24},{1,9},{9,1},{17,25},{2,10},{10,2},{18,26},{3,1... | collective-permute-start | bytes 3145736 | tf_op jit(solution)/shard_map/ppermute | solution.py:344
  38.6 5.6 %collective-permute-start = (bf16[2,4,4,128,128]{4,3,2,1,0:T(8,128)(2,1)S(1)}, bf16[2,4,4,128,128]{4,3,2,1,0:T(8,128)(2,1)S(1)}, u32[]{:S(2)}, u32[]{:S(2)}) collective-permute-start(bf16[2,4,4,128,128]{4,3,2,1,0:T(8,128)(2,1)S(1)} %bitcast.71), channel_id=1, source_target_pairs={{0,8},{1,9},{2,10},{3,11},{4,12},{5,13},{6,14},{7,15}} | collective-permute-start | bytes 3145736 | tf_op jit(solution)/shard_map/ppermute | solution.py:345
  41.3 15.6 %collective-permute-start.6 = (bf16[4,4,128,128]{3,2,1,0:T(8,128)(2,1)S(1)}, bf16[4,4,128,128]{3,2,1,0:T(8,128)(2,1)S(1)}, u32[]{:S(2)}, u32[]{:S(2)}) collective-permute-start(bf16[4,4,128,128]{3,2,1,0:T(8,128)(2,1)S(1)} %fusion.3), channel_id=1, source_target_pairs={{0,1},{1,0},{2,3},{3,2},{4,5},{5,4},{6,7},{7,6},{8,9},{9,8},{10,11... | collective-permute-start | bytes 1572872 | tf_op jit(solution)/shard_map/ppermute | solution.py:333
  44.7 23.0 %collective-permute-start.1 = (bf16[4,4,128,128]{3,2,1,0:T(8,128)(2,1)S(1)}, bf16[4,4,128,128]{3,2,1,0:T(8,128)(2,1)S(1)}, u32[]{:S(2)}, u32[]{:S(2)}) collective-permute-start(bf16[4,4,128,128]{3,2,1,0:T(8,128)(2,1)S(1)} %fusion.2), channel_id=1, source_target_pairs={{0,1},{1,0},{2,3},{3,2},{4,5},{5,4},{6,7},{7,6},{8,9},{9,8},{10,11... | collective-permute-start | bytes 1572872 | tf_op jit(solution)/shard_map/ppermute | solution.py:333
  57.2 10.7 %collective-permute-start.7 = (bf16[4,128,128]{2,1,0:T(8,128)(2,1)S(1)}, bf16[4,128,128]{2,1,0:T(8,128)(2,1)S(1)}, u32[]{:S(2)}, u32[]{:S(2)}) collective-permute-start(bf16[4,128,128]{2,1,0:T(8,128)(2,1)S(1)} %get-tuple-element.16), channel_id=1, source_target_pairs={{0,2},{1,3},{2,0},{3,1},{4,6},{5,7},{6,4},{7,5},{8,10},{9,11},{10,... | collective-permute-start | bytes 393224 | tf_op jit(solution)/shard_map/ppermute | solution.py:333
  59.3 8.7 %collective-permute-start.9 = (bf16[4,128,128]{2,1,0:T(8,128)(2,1)S(1)}, bf16[4,128,128]{2,1,0:T(8,128)(2,1)S(1)}, u32[]{:S(2)}, u32[]{:S(2)}) collective-permute-start(bf16[4,128,128]{2,1,0:T(8,128)(2,1)S(1)} %get-tuple-element.17), channel_id=1, source_target_pairs={{0,6},{1,7},{2,4},{3,5},{4,2},{5,3},{6,0},{7,1},{8,14},{9,15},{10,... | collective-permute-start | bytes 393224 | tf_op jit(solution)/shard_map/ppermute | solution.py:333
  61.9 10.4 %collective-permute-start.8 = (bf16[4,128,128]{2,1,0:T(8,128)(2,1)S(1)}, bf16[4,128,128]{2,1,0:T(8,128)(2,1)S(1)}, u32[]{:S(2)}, u32[]{:S(2)}) collective-permute-start(bf16[4,128,128]{2,1,0:T(8,128)(2,1)S(1)} %get-tuple-element.18), channel_id=1, source_target_pairs={{0,4},{1,5},{2,6},{3,7},{4,0},{5,1},{6,2},{7,3},{8,12},{9,13},{10,... | collective-permute-start | bytes 393224 | tf_op jit(solution)/shard_map/ppermute | solution.py:333
  72.3 21.0 %collective-permute-start.10 = (f32[4,128,128]{2,1,0:T(8,128)S(1)}, f32[4,128,128]{2,1,0:T(8,128)S(1)}, u32[]{:S(2)}, u32[]{:S(2)}) collective-permute-start(f32[4,128,128]{2,1,0:T(8,128)S(1)} %fusion.6), channel_id=1, source_target_pairs={{0,16},{8,24},{1,17},{9,25},{2,18},{10,26},{3,19},{11,27},{4,20},{... | collective-permute-start | bytes 786440 | tf_op jit(solution)/shard_map/ppermute | solution.py:348
  75.7 9.2 %collective-permute-start.2 = (bf16[4,128,128]{2,1,0:T(8,128)(2,1)S(1)}, bf16[4,128,128]{2,1,0:T(8,128)(2,1)S(1)}, u32[]{:S(2)}, u32[]{:S(2)}) collective-permute-start(bf16[4,128,128]{2,1,0:T(8,128)(2,1)S(1)} %get-tuple-element.13), channel_id=1, source_target_pairs={{0,2},{1,3},{2,0},{3,1},{4,6},{5,7},{6,4},{7,5},{8,10},{9,11},{10,... | collective-permute-start | bytes 393224 | tf_op jit(solution)/shard_map/ppermute | solution.py:333
  77.7 8.9 %collective-permute-start.4 = (bf16[4,128,128]{2,1,0:T(8,128)(2,1)S(1)}, bf16[4,128,128]{2,1,0:T(8,128)(2,1)S(1)}, u32[]{:S(2)}, u32[]{:S(2)}) collective-permute-start(bf16[4,128,128]{2,1,0:T(8,128)(2,1)S(1)} %get-tuple-element.14), channel_id=1, source_target_pairs={{0,6},{1,7},{2,4},{3,5},{4,2},{5,3},{6,0},{7,1},{8,14},{9,15},{10,... | collective-permute-start | bytes 393224 | tf_op jit(solution)/shard_map/ppermute | solution.py:333
  82.2 11.1 %collective-permute-start.3 = (bf16[4,128,128]{2,1,0:T(8,128)(2,1)S(1)}, bf16[4,128,128]{2,1,0:T(8,128)(2,1)S(1)}, u32[]{:S(2)}, u32[]{:S(2)}) collective-permute-start(bf16[4,128,128]{2,1,0:T(8,128)(2,1)S(1)} %get-tuple-element.15), channel_id=1, source_target_pairs={{0,4},{1,5},{2,6},{3,7},{4,0},{5,1},{6,2},{7,3},{8,12},{9,13},{10,... | collective-permute-start | bytes 393224 | tf_op jit(solution)/shard_map/ppermute | solution.py:333

commit v2 on v1

v2 whole, which is shorter than its diff:
```python
import functools

import jax
import jax.numpy as jnp
from jax import lax
from jax.experimental import pallas as pl
from jax.experimental.pallas import tpu as pltpu
from jax.sharding import PartitionSpec as P

LANES = 128
GROUP = 4
RING = 7
WIDE = 4
LEAD = 2
WINDOW = 5
F32 = jnp.float32
BF16 = jnp.bfloat16


def iota(shape, dim):
    return lax.broadcasted_iota(jnp.int32, shape, dim)


def dot(a, b):
    return jnp.dot(a, b, preferred_element_type=F32)


def dot_t(a, b):
    return lax.dot_general(a, b, (((1,), (1,)), ((), ())), preferred_element_type=F32)


def kernel(
    feats,
    relative,
    pos_ref,
    ids_hbm,
    res_hbm,
    enc_hbm,
    dec_hbm,
    keep_early,
    send_early,
    keep_late,
    send_late,
    ids_v,
    lo_v,
    sh_v,
    bits_v,
    rank_v,
    res_v,
    enc_v,
    list_v,
    list_s,
    acts_v,
    lhs_v,
    buf,
    acc,
    out_v,
    small_sem,
    enc_sem,
    dec_sem,
    out_sem,
):
    tokens, width = res_v.shape
    shard = acts_v.shape[1]
    slots = list_v.shape[1]
    rows_hi = shard // LANES
    max_blocks = slots // LANES
    ring = buf.shape[0]
    wides = acc.shape[1]
    section_pos, feat_pos = pos_ref[0], pos_ref[1]
    core = section_pos % 2

    ids_copy = pltpu.make_async_copy(ids_hbm, ids_v, small_sem.at[0])
    ids_copy.start()
    res_copy = pltpu.make_async_copy(res_hbm, res_v, small_sem.at[1])
    res_copy.start()
    chunk = min(4 * LANES, shard)
    chunks = shard // chunk

    def enc_copy(i):
        columns = pl.ds(i * chunk, chunk) if isinstance(i, int) else pl.ds(pl.multiple_of(i * chunk, chunk), chunk)
        return pltpu.make_async_copy(enc_hbm.at[:, columns], enc_v.at[i], enc_sem.at[i])

    early = (chunks + 1) // 2
    for i in range(early):
        enc_copy(i).start()

    ids_copy.wait()
    local = ids_v[...] - feat_pos * shard
    inside = (local >= 0) & (local < shard)
    lo_v[...] = jnp.where(inside, local & (LANES - 1), -1)
    sh_v[...] = jnp.where(inside, jnp.left_shift(1, (local >> 7) & 31), 0)
    lane_of = iota((LANES, tokens), 0)

    def gather_bits(k, bits):
        hit = lo_v[pl.ds(k, 1), :] == lane_of
        return bits | jnp.where(hit, sh_v[pl.ds(k, 1), :], 0)

    bits_t = lax.fori_loop(0, ids_v.shape[0], gather_bits, jnp.zeros((LANES, tokens), jnp.int32), unroll=8)
    bits = bits_t.T
    bits_v[...] = bits
    union = bits
    while union.shape[0] > 1:
        half = union.shape[0] // 2
        union = union[:half] | union[half:]

    rows = 16 * (-(-rows_hi // 16))
    hi_of = iota((rows, LANES), 0)
    flags = jnp.where(hi_of < rows_hi, jnp.right_shift(jnp.broadcast_to(union, (rows, LANES)), hi_of & 31) & 1, 0)
    flags_f = flags.astype(F32)
    upper = (iota((LANES, LANES), 0) <= iota((LANES, LANES), 1)).astype(F32).astype(BF16)
    inclusive = dot(flags_f.astype(BF16), upper)
    row_total = jnp.broadcast_to(jnp.sum(flags_f, axis=1, keepdims=True), (rows, LANES))
    below = (iota((rows, rows), 1) < iota((rows, rows), 0)).astype(F32).astype(BF16)
    row_start = dot(below, row_total.astype(BF16))
    row_end = row_start + row_total
    count = jnp.sum(flags_f).astype(jnp.int32)
    rank_v[...] = jnp.where(flags > 0, row_start + inclusive - 1.0, -1.0)

    slot = iota((rows, slots), 1).astype(F32)
    start_w = jnp.concatenate([row_start] * max_blocks, axis=1)
    end_w = jnp.concatenate([row_end] * max_blocks, axis=1)
    in_row = (start_w <= slot) & (slot < end_w)
    in_row_f = in_row.astype(F32)
    row_of = jnp.sum(in_row_f * iota((rows, slots), 0).astype(F32), axis=0, keepdims=True)
    place = jnp.sum(jnp.where(in_row, slot - start_w, 0.0), axis=0, keepdims=True)
    tall = jnp.concatenate([inclusive, jnp.zeros((LANES - rows, LANES), F32)], axis=0) if rows < LANES else inclusive
    prefix = dot(tall.T[:, :rows].astype(BF16), in_row_f.astype(BF16))
    lane_in = jnp.sum((prefix <= place).astype(F32), axis=0, keepdims=True)
    latent = row_of * float(LANES) + lane_in
    slot_row = iota((1, slots), 1)
    list_v[...] = jnp.where(slot_row < count, latent.astype(jnp.int32), slot_row)
    list_copy = pltpu.make_async_copy(list_v, list_s, small_sem.at[2])
    list_copy.start()
    blocks = jnp.maximum(1, (count + (LANES - 1)) // LANES)
    groups = (blocks + (GROUP - 1)) // GROUP

    def gather(place, base, i):
        pltpu.make_async_copy(
            dec_hbm.at[list_s[0, base + i]],
            buf.at[place, :, :, pl.ds(pl.multiple_of(2 * i, 2), 2), :],
            dec_sem.at[place],
        ).start()

    def issue(block, carry):
        place = lax.rem(block, ring)

        def row(i, carry):
            gather(place, block * LANES, i)
            return carry

        return lax.fori_loop(0, LANES, row, carry, unroll=True)

    def encode(i):
        enc_copy(i).wait()
        pre = dot(res_v[...], enc_v[i])
        for q in range(chunk // LANES):
            hi = i * (chunk // LANES) + q
            active = (jnp.right_shift(bits_v[...], hi) & 1) > 0
            piece = jnp.maximum(pre[:, q * LANES : (q + 1) * LANES], 0.0)
            acts_v[:, pl.ds(pl.multiple_of(hi * LANES, LANES), LANES)] = jnp.where(active, piece, 0.0).astype(BF16)

    def encode_step(i, carry):
        encode(i)
        return carry

    res_copy.wait()
    for i in range(early, chunks):
        enc_copy(i).start()
    first_blocks = jnp.minimum(blocks, ring)
    lead = jnp.minimum(blocks, LEAD)
    lax.fori_loop(0, early, encode_step, 0)
    list_copy.wait()
    lax.fori_loop(0, lead, issue, 0)
    lax.fori_loop(early, chunks, encode_step, 0)
    lax.fori_loop(lead, first_blocks, issue, 0)

    twice = ((iota((LANES, 2 * LANES), 1) >> 1) == iota((LANES, 2 * LANES), 0)).astype(F32).astype(BF16)
    parity = iota((tokens, 2 * LANES), 1) & 1
    window = min(WINDOW, rows_hi)

    def row_at(slot):
        return list_s[0, jnp.clip(slot, 0, jnp.maximum(count - 1, 0))] >> 7

    def compact(b, start, many):
        want = (iota((LANES, LANES), 0) + b * LANES).astype(F32)
        chosen = jnp.concatenate(
            [(rank_v[pl.ds(start + q, 1), :] == want).astype(F32).astype(BF16) for q in range(many)], axis=1
        )
        from_acts = acts_v[:, pl.ds(pl.multiple_of(start * LANES, LANES), many * LANES)]
        picked = dot_t(from_acts, chosen).astype(BF16)
        doubled = dot(picked, twice)
        lhs_v[b, :tokens, :] = jnp.where(parity == core, doubled, 0.0).astype(BF16)
        lhs_v[b, tokens:, :] = jnp.where(parity == core, 0.0, doubled).astype(BF16)

    def compact_wide(b, carry):
        compact(b, 0, rows_hi)
        return carry

    starts = [jnp.minimum(row_at(b * LANES), rows_hi - window) for b in range(ring)]
    narrow_fits = blocks >= ring
    for b in range(ring):
        narrow_fits = narrow_fits & (row_at(b * LANES + LANES - 1) < starts[b] + window)

    @pl.when(narrow_fits)
    def _():
        for b in range(ring):
            compact(b, starts[b], window)

    lax.fori_loop(jnp.where(narrow_fits, ring, 0), blocks, compact_wide, 0)

    outs = {(0, 0): keep_early, (0, 1): send_early, (1, 0): keep_late, (1, 1): send_late}

    def out_copy(pair, part, wide, dest):
        return pltpu.make_async_copy(out_v.at[pair, wide, part], outs[pair, part].at[dest], out_sem)

    def multiply(group, size, first, last):
        places = [lax.rem(group * GROUP + b, ring) for b in range(size)]
        for place in places:
            pltpu.make_async_copy(buf.at[place], buf.at[place], dec_sem.at[place]).wait()
        left = jnp.concatenate([lhs_v[group * GROUP + b] for b in range(size)], axis=1)
        for pair in (1, 0):

            def wide_step(wide, carry):
                right = jnp.concatenate(
                    [
                        jnp.concatenate([buf[place, wide * WIDE + q, pair] for q in range(WIDE)], axis=1)
                        for place in places
                    ],
                    axis=0,
                )
                total = dot(left, right)
                if not first:
                    total = total + acc[pair, wide]
                if last:
                    narrow = total.astype(BF16)
                    for part in range(2):
                        for q in range(WIDE):
                            out_v[pair, wide, part, q] = narrow[
                                part * tokens : (part + 1) * tokens, q * LANES : (q + 1) * LANES
                            ]
                else:
                    acc[pair, wide] = total
                return carry

            lax.fori_loop(0, wides, wide_step, 0, unroll=True)
            if last:
                for wide in range(wides):
                    if relative:
                        apart = jnp.bitwise_xor(wide, feat_pos)
                        dest = (apart & 1) * (feats // 2) + (apart >> 1)
                    else:
                        dest = wide
                    for part in range(2):
                        out_copy(pair, part, wide, dest).start()

    def each_group(group, carry):
        here = blocks - group * GROUP
        for first in (True, False):
            at = (group == 0) if first else (group > 0)
            if max_blocks > GROUP:

                @pl.when(at & (here > GROUP))
                def _():
                    multiply(group, GROUP, first, False)

            elif not first:
                continue
            for size in range(1, min(GROUP, max_blocks) + 1):

                @pl.when(at & (here == size))
                def _():
                    multiply(group, size, first, True)

        if max_blocks > ring:
            done = (group + 1) * GROUP
            lax.fori_loop(jnp.minimum(blocks, done - GROUP + ring), jnp.minimum(blocks, done + ring), issue, 0)

        return carry

    lax.fori_loop(0, groups, each_group, 0)
    for pair in range(2):
        for wide in range(wides):
            for part in range(2):
                out_copy(pair, part, wide, 0).wait()


def partial_sums(position, ids, residual, enc, dec, feats, relative):
    tokens, width = residual.shape
    shard = enc.shape[1]
    tiles = width // LANES
    wides = tiles // WIDE
    max_blocks = -(-shard // LANES)
    slots = max_blocks * LANES
    ring = min(RING, max_blocks)
    rows = 16 * (-(-max_blocks // 16))
    chunks = shard // min(4 * LANES, shard)
    return pl.pallas_call(
        functools.partial(kernel, feats, relative),
        out_shape=[jax.ShapeDtypeStruct((wides, WIDE, tokens, LANES), BF16)] * 4,
        in_specs=[pl.BlockSpec(memory_space=pltpu.SMEM)] + [pl.BlockSpec(memory_space=pl.ANY)] * 4,
        out_specs=[pl.BlockSpec(memory_space=pl.ANY)] * 4,
        scratch_shapes=[
            pltpu.VMEM(ids.shape, jnp.int32),
            pltpu.VMEM(ids.shape, jnp.int32),
            pltpu.VMEM(ids.shape, jnp.int32),
            pltpu.VMEM((tokens, LANES), jnp.int32),
            pltpu.VMEM((rows, LANES), F32),
            pltpu.VMEM((tokens, width), BF16),
            pltpu.VMEM((chunks, width, shard // chunks), BF16),
            pltpu.VMEM((1, slots), jnp.int32),
            pltpu.SMEM((1, slots), jnp.int32),
            pltpu.VMEM((tokens, shard), BF16),
            pltpu.VMEM((max_blocks, 2 * tokens, 2 * LANES), BF16),
            pltpu.VMEM((ring, tiles, 2, 2 * LANES, LANES), BF16),
            pltpu.VMEM((2, wides, 2 * tokens, WIDE * LANES), F32),
            pltpu.VMEM((2, wides, 2, WIDE, tokens, LANES), BF16),
            pltpu.SemaphoreType.DMA((3,)),
            pltpu.SemaphoreType.DMA((chunks,)),
            pltpu.SemaphoreType.DMA((ring,)),
            pltpu.SemaphoreType.DMA,
        ],
        compiler_params=pltpu.CompilerParams(vmem_limit_bytes=62 * 2**20),
        cost_estimate=pl.CostEstimate(
            flops=4 * tokens * width * shard, bytes_accessed=2 * width * shard * 3, transcendentals=0
        ),
    )(position, ids, residual, enc, dec)


def local(residual, enc_weight, dec_weight, latent_ids):
    feats = lax.axis_size("feat")
    section_pos = lax.axis_index("section")
    feat_pos = lax.axis_index("feat")
    tokens, width = residual.shape[1:]
    shard = enc_weight.shape[2]
    tiles = width // LANES
    own = width // feats
    relative = own == WIDE * LANES
    position = jnp.stack([section_pos, feat_pos]).astype(jnp.int32)
    ids = latent_ids[0].T
    dec = dec_weight[0].reshape(shard, 2, 2, tiles, LANES).transpose(0, 3, 1, 2, 4)
    sums = partial_sums(position, ids, residual[0], enc_weight[0], dec, feats, relative)

    def blocks_of(part):
        if relative:
            return part.reshape(2, feats // 2, own, LANES)
        part = jnp.transpose(part, (0, 1, 3, 2)).reshape(feats, own, tokens)
        apart = jnp.arange(feats)
        apart = (apart % (feats // 2)) * 2 + apart // (feats // 2)
        return jnp.take(part, apart ^ feat_pos, axis=0).reshape(2, feats // 2, own, tokens)

    keep_early, send_early, keep_late, send_late = (blocks_of(part) for part in sums)
    everyone, low = (0, 1, 2, 3), (0, 1)

    def across_feat(x, bits, sections):
        pairs = [(s * feats + f, s * feats + (f ^ bits)) for s in sections for f in range(feats)]
        return lax.ppermute(x, ("section", "feat"), pairs)

    def halve(x, sections):
        return x[0] + across_feat(x[1].astype(BF16), 1, sections).astype(F32)

    def finish(x, sections):
        narrow = x.astype(BF16)
        total = x[0]
        for device in range(1, feats // 2):
            total = total + across_feat(narrow[device], 2 * device, sections).astype(F32)
        return total

    late = keep_late.astype(F32) + lax.ppermute(send_late, "section", [(0, 1), (1, 0), (2, 3)]).astype(F32)
    early = keep_early.astype(F32) + lax.ppermute(send_early, "section", [(0, 1)]).astype(F32)
    half = own // 2
    is_low = section_pos < 2
    crossed = lax.ppermute(late[:, :, :half].astype(BF16), "section", [(0, 2), (1, 3)]).astype(F32)
    second_late = finish(halve(late[:, :, half:], everyone), everyone)
    first = finish(halve(jnp.where(is_low, early[:, :, :half], late[:, :, :half] + crossed), everyone), everyone)
    second_early = finish(halve(early[:, :, half:], low), low)
    carried = lax.ppermute(second_late, "section", [(0, 2), (1, 3)])
    written = jnp.concatenate([first, jnp.where(is_low, second_early, second_late + carried)], axis=0)
    if relative:
        written = jnp.transpose(written.reshape(WIDE, tokens, LANES), (0, 2, 1)).reshape(own, tokens)
    return written.astype(BF16)[None]


def solution(mesh):
    in_specs = (
        P("section", None, None),
        P("section", None, "feat"),
        P("section", "feat", None, None),
        P("section", None, None),
    )
    out_specs = P("section", "feat", None)
    return jax.shard_map(local, mesh=mesh, in_specs=in_specs, out_specs=out_specs, check_vma=False)
```

time: 94.5 us -> 71.5 us (0.76)
  waiting for transfers between devices: 27.5 us -> 11.5 us
  Pallas kernels: 32.8 us -> 21.2 us
  starting transfers between devices: 28.1 us -> 34.4 us
  local copies, waits for them, and re-layouts: 3.76 us -> 1.01 us
  other arithmetic: 1.89 us -> 2.87 us
    ppermute x8 -> x12, waiting for transfers between devices: 27.2 us -> 11 us  [across_feat(): return lax.ppermute(x, ('section', 'feat'), pairs)]
    pallas_call x1, Pallas kernels: 32.8 us -> 21.2 us  [partial_sums(): pl.pallas_call(functools.partial(kernel, feats, relative), out_shape=[jax...]
    ppermute x8 -> x12, starting transfers between devices: 20.4 us -> 24.5 us  [across_feat(): return lax.ppermute(x, ('section', 'feat'), pairs)]
    slice x1, local copies, waits for them, and re-layouts: 2.75 us -> 0.08 us  [local(): late[:, :, :half] + crossed]
    ppermute x3 -> x4, starting transfers between devices: 7.75 us -> 9.85 us  [the longest x1 4.16 us: local(): lax.ppermute(late[:, :, :half].astype(BF16), 'section', [(0, 2), (1, 3)])]
    add x3, other arithmetic: 0.74 us -> 1.76 us  [the longest x1 1.52 us: local(): keep_late.astype(F32)]
  transfers between devices with their start and end apart: 11 -> 16, of which waited for: 7 -> 5; matrix products, arithmetic and copies ran while one was open for 1% -> 3% of each run, Pallas kernels for 0% -> 0%
where the time goes in v2:
time: 71.5 us; the launch traced here: 71.2 us
  starting transfers between devices  34.4 us (48%)
  Pallas kernels  21.2 us (30%)
  waiting for transfers between devices  11.5 us (16%)
  other arithmetic  2.87 us (4%)
  local copies, waits for them, and re-layouts  1.01 us (1%)
    ppermute x12, starting transfers between devices, across_feat(): return lax.ppermute(x, ('section', 'feat'), pairs)  24.5 us
    pallas_call x1, Pallas kernels, partial_sums(): pl.pallas_call(functools.partial(kernel, feats, relative), out_shape=[jax...  21.2 us
    ppermute x12, waiting for transfers between devices, across_feat(): return lax.ppermute(x, ('section', 'feat'), pairs)  11 us
    ppermute x1, starting transfers between devices, local(): lax.ppermute(late[:, :, :half].astype(BF16), 'section', [(0, 2), (1, 3)])  4.16 us
    ppermute x1, starting transfers between devices, local(): lax.ppermute(send_late, 'section', [(0, 1), (1, 0), (2, 3)]).astype(F32)  2.38 us
    ppermute x1, starting transfers between devices, local(): lax.ppermute(send_early, 'section', [(0, 1)]).astype(F32)  2.01 us
    add x1, other arithmetic, local(): keep_late.astype(F32)  1.52 us
  transfers between devices with their start and end apart: 16, of which 5 were waited for; matrix products, arithmetic and copies ran while one was open for 3% of the time, Pallas kernels for 0%

profile of v2, /device:TPU:0, one launch (start us, length us, event | category | flops | bytes accessed | tf_op | source)
XLA Modules:
  0.0 71.2 jit_solution(1407471294328101246)
XLA Ops:
  0.0 0.6 pad_add_fusion.pos_ref
  0.6 21.2 %shard_map.46 = (bf16[8,4,128,128]{3,2,1,0:T(8,128)(2,1)}, bf16[8,4,128,128]{3,2,1,0:T(8,128)(2,1)}, bf16[8,4,128,128]{3,2,1,0:T(8,128)(2,1)}, bf16[8,4,128,128]{3,2,1,0:T(8,128)(2,1)}) custom-call(s32[2]{0:T(128)} %pad_add_fusion.pos_ref, s32[64,128]{1,0:T(8,128)} %bitcast.94, bf16[128,4096]{1,0:T(8,128)(2,1)} %bitcast.90, bf16[4096,2048]{1,0:T(8,128)(2,1)} %bitcast.89, ...), custom_call_target="tpu_custom_call" | custom-call | flops 4294967296 | bytes 50331648 | tf_op jit(solution)/shard_map/pallas_call | solution.py:298
  21.9 2.4 %collective-permute-start.1 = (bf16[2,4,512,128]{3,2,1,0:T(8,128)(2,1)}, bf16[2,4,512,128]{3,2,1,0:T(8,128)(2,1)S(1)}, u32[]{:S(2)}, u32[]{:S(2)}) collective-permute-start(bf16[2,4,512,128]{3,2,1,0:T(8,128)(2,1)} %bitcast.96), channel_id=1, source_target_pairs={{0,8},{8,0},{16,24},{1,9},{9,1},{17,25},{2,10},{10,2},{18,26},{3,1... | collective-permute-start | bytes 3145736 | tf_op jit(solution)/shard_map/ppermute | solution.py:369
  24.3 2.0 %collective-permute-start = (bf16[2,4,512,128]{3,2,1,0:T(8,128)(2,1)}, bf16[2,4,512,128]{3,2,1,0:T(8,128)(2,1)S(1)}, u32[]{:S(2)}, u32[]{:S(2)}) collective-permute-start(bf16[2,4,512,128]{3,2,1,0:T(8,128)(2,1)} %bitcast.95), channel_id=1, source_target_pairs={{0,8},{1,9},{2,10},{3,11},{4,12},{5,13},{6,14},{7,15}} | collective-permute-start | bytes 3145736 | tf_op jit(solution)/shard_map/ppermute | solution.py:370
  26.3 0.5 collective-permute-done.1
  26.8 1.5 %convert_add_fusion = f32[2,4,512,128]{3,2,1,0:T(8,128)S(1)} fusion(bf16[2,4,512,128]{3,2,1,0:T(8,128)(2,1)} %bitcast.92, bf16[2,4,512,128]{3,2,1,0:T(8,128)(2,1)S(1)} %collective-permute-done.1), kind=kLoop, calls=%fused_computation | loop fusion | flops 1572864 | bytes 4194304 | tf_op jit(solution)/shard_map/add | solution.py:369
  28.3 0.1 slice.167
  28.4 4.2 %collective-permute-start.2 = (bf16[2,4,256,128]{3,2,1,0:T(8,128)(2,1)S(1)}, bf16[2,4,256,128]{3,2,1,0:T(8,128)(2,1)S(1)}, u32[]{:S(2)}, u32[]{:S(2)}) collective-permute-start(bf16[2,4,256,128]{3,2,1,0:T(8,128)(2,1)S(1)} %slice.167), channel_id=1, source_target_pairs={{0,16},{8,24},{1,17},{9,25},{2,18},{10,26},{3,19},{11,27},{4,20},{... | collective-permute-start | bytes 1572872 | tf_op jit(solution)/shard_map/ppermute | solution.py:373
  32.6 1.5 %collective-permute-start.11 = (bf16[4,256,128]{2,1,0:T(8,128)(2,1)S(1)}, bf16[4,256,128]{2,1,0:T(8,128)(2,1)S(1)}, u32[]{:S(2)}, u32[]{:S(2)}) collective-permute-start(bf16[4,256,128]{2,1,0:T(8,128)(2,1)S(1)} %fusion.5), channel_id=1, source_target_pairs={{0,1},{1,0},{2,3},{3,2},{4,5},{5,4},{6,7},{7,6},{8,9},{9,8},{10,11... | collective-permute-start | bytes 786440 | tf_op jit(solution)/shard_map/ppermute | solution.py:357
  34.1 0.2 convert_add_fusion.1
  34.3 2.5 %collective-permute-start.7 = (bf16[4,256,128]{2,1,0:T(8,128)(2,1)S(1)}, bf16[4,256,128]{2,1,0:T(8,128)(2,1)S(1)}, u32[]{:S(2)}, u32[]{:S(2)}) collective-permute-start(bf16[4,256,128]{2,1,0:T(8,128)(2,1)S(1)} %fusion.4), channel_id=1, source_target_pairs={{0,1},{1,0},{2,3},{3,2},{4,5},{5,4},{6,7},{7,6},{8,9},{9,8},{10,11... | collective-permute-start | bytes 786440 | tf_op jit(solution)/shard_map/ppermute | solution.py:357
  36.8 5.0 %collective-permute-done.11 = bf16[4,256,128]{2,1,0:T(8,128)(2,1)S(1)} collective-permute-done((bf16[4,256,128]{2,1,0:T(8,128)(2,1)S(1)}, bf16[4,256,128]{2,1,0:T(8,128)(2,1)S(1)}, u32[]{:S(2)}, u32[]{:S(2)}) %collective-permute-start.11) | collective-permute-done | bytes 262176 | tf_op jit(solution)/shard_map/ppermute | solution.py:357
  41.8 0.1 fusion.22
  41.9 1.6 %collective-permute-start.12 = (bf16[256,128]{1,0:T(8,128)(2,1)S(1)}, bf16[256,128]{1,0:T(8,128)(2,1)S(1)}, u32[]{:S(2)}, u32[]{:S(2)}) collective-permute-start(bf16[256,128]{1,0:T(8,128)(2,1)S(1)} %get-tuple-element.25), channel_id=1, source_target_pairs={{0,2},{1,3},{2,0},{3,1},{4,6},{5,7},{6,4},{7,5},{8,10},{9,11},{10,... | collective-permute-start | bytes 196616 | tf_op jit(solution)/shard_map/ppermute | solution.py:357
  43.5 2.5 %collective-permute-start.13 = (bf16[256,128]{1,0:T(8,128)(2,1)S(1)}, bf16[256,128]{1,0:T(8,128)(2,1)S(1)}, u32[]{:S(2)}, u32[]{:S(2)}) collective-permute-start(bf16[256,128]{1,0:T(8,128)(2,1)S(1)} %get-tuple-element.27), channel_id=1, source_target_pairs={{0,4},{1,5},{2,6},{3,7},{4,0},{5,1},{6,2},{7,3},{8,12},{9,13},{10,... | collective-permute-start | bytes 196616 | tf_op jit(solution)/shard_map/ppermute | solution.py:357
  46.1 0.3 collective-permute-start.14
  46.4 0.2 collective-permute-done.7
  46.6 0.1 fusion.20
  46.6 0.1 slice_select_fusion
  46.8 1.5 %collective-permute-start.3 = (bf16[4,256,128]{2,1,0:T(8,128)(2,1)S(1)}, bf16[4,256,128]{2,1,0:T(8,128)(2,1)S(1)}, u32[]{:S(2)}, u32[]{:S(2)}) collective-permute-start(bf16[4,256,128]{2,1,0:T(8,128)(2,1)S(1)} %fusion.3), channel_id=1, source_target_pairs={{0,1},{1,0},{2,3},{3,2},{4,5},{5,4},{6,7},{7,6},{8,9},{9,8},{10,11... | collective-permute-start | bytes 786440 | tf_op jit(solution)/shard_map/ppermute | solution.py:357
  48.3 5.6 %collective-permute-start.10 = (bf16[256,128]{1,0:T(8,128)(2,1)S(1)}, bf16[256,128]{1,0:T(8,128)(2,1)S(1)}, u32[]{:S(2)}, u32[]{:S(2)}) collective-permute-start(bf16[256,128]{1,0:T(8,128)(2,1)S(1)} %get-tuple-element.23), channel_id=1, source_target_pairs={{0,6},{1,7},{2,4},{3,5},{4,2},{5,3},{6,0},{7,1},{8,14},{9,15},{10,... | collective-permute-start | bytes 196616 | tf_op jit(solution)/shard_map/ppermute | solution.py:357
  54.0 1.9 %collective-permute-start.8 = (bf16[256,128]{1,0:T(8,128)(2,1)S(1)}, bf16[256,128]{1,0:T(8,128)(2,1)S(1)}, u32[]{:S(2)}, u32[]{:S(2)}) collective-permute-start(bf16[256,128]{1,0:T(8,128)(2,1)S(1)} %get-tuple-element.22), channel_id=1, source_target_pairs={{0,2},{1,3},{2,0},{3,1},{4,6},{5,7},{6,4},{7,5},{8,10},{9,11},{10,... | collective-permute-start | bytes 196616 | tf_op jit(solution)/shard_map/ppermute | solution.py:357
  55.9 2.6 %collective-permute-start.9 = (bf16[256,128]{1,0:T(8,128)(2,1)S(1)}, bf16[256,128]{1,0:T(8,128)(2,1)S(1)}, u32[]{:S(2)}, u32[]{:S(2)}) collective-permute-start(bf16[256,128]{1,0:T(8,128)(2,1)S(1)} %get-tuple-element.24), channel_id=1, source_target_pairs={{0,4},{1,5},{2,6},{3,7},{4,0},{5,1},{6,2},{7,3},{8,12},{9,13},{10,... | collective-permute-start | bytes 196616 | tf_op jit(solution)/shard_map/ppermute | solution.py:357
  58.5 1.3 %collective-permute-start.15 = (f32[256,128]{1,0:T(8,128)S(1)}, f32[256,128]{1,0:T(8,128)S(1)}, u32[]{:S(2)}, u32[]{:S(2)}) collective-permute-start(f32[256,128]{1,0:T(8,128)S(1)} %fusion.8), channel_id=1, source_target_pairs={{0,16},{8,24},{1,17},{9,25},{2,18},{10,26},{3,19},{11,27},{4,20},{... | collective-permute-start | bytes 393224 | tf_op jit(solution)/shard_map/ppermute | solution.py:377
  59.9 0.1 fusion.18
  60.0 1.4 %collective-permute-start.4 = (bf16[256,128]{1,0:T(8,128)(2,1)S(1)}, bf16[256,128]{1,0:T(8,128)(2,1)S(1)}, u32[]{:S(2)}, u32[]{:S(2)}) collective-permute-start(bf16[256,128]{1,0:T(8,128)(2,1)S(1)} %get-tuple-element.19), channel_id=1, source_target_pairs={{0,2},{1,3},{2,0},{3,1},{4,6},{5,7},{6,4},{7,5},{8,10},{9,11},{10,... | collective-permute-start | bytes 196616 | tf_op jit(solution)/shard_map/ppermute | solution.py:357
  61.4 2.9 %collective-permute-start.5 = (bf16[256,128]{1,0:T(8,128)(2,1)S(1)}, bf16[256,128]{1,0:T(8,128)(2,1)S(1)}, u32[]{:S(2)}, u32[]{:S(2)}) collective-permute-start(bf16[256,128]{1,0:T(8,128)(2,1)S(1)} %get-tuple-element.21), channel_id=1, source_target_pairs={{0,4},{1,5},{2,6},{3,7},{4,0},{5,1},{6,2},{7,3},{8,12},{9,13},{10,... | collective-permute-start | bytes 196616 | tf_op jit(solution)/shard_map/ppermute | solution.py:357
  64.3 0.1 collective-permute-start.6
  64.4 0.1 fusion.13
  64.5 3.5 %collective-permute-done.5 = bf16[256,128]{1,0:T(8,128)(2,1)S(1)} collective-permute-done((bf16[256,128]{1,0:T(8,128)(2,1)S(1)}, bf16[256,128]{1,0:T(8,128)(2,1)S(1)}, u32[]{:S(2)}, u32[]{:S(2)}) %collective-permute-start.5) | collective-permute-done | bytes 65568 | tf_op jit(solution)/shard_map/ppermute | solution.py:357
  68.0 2.4 %collective-permute-done.6 = bf16[256,128]{1,0:T(8,128)(2,1)S(1)} collective-permute-done((bf16[256,128]{1,0:T(8,128)(2,1)S(1)}, bf16[256,128]{1,0:T(8,128)(2,1)S(1)}, u32[]{:S(2)}, u32[]{:S(2)}) %collective-permute-start.6) | collective-permute-done | bytes 65568 | tf_op jit(solution)/shard_map/ppermute | solution.py:357
  70.4 0.8 %copy.5 = bf16[4,128,128]{1,2,0:T(8,128)(2,1)} copy(bf16[4,128,128]{2,1,0:T(8,128)(2,1)S(1)} %bitcast.93) | data formatting | bytes 262144 | tf_op jit(solution)/shard_map/convert_element_type | solution.py:381
  (22 shorter events, 0.3 us)
Async XLA Ops:
  21.9 4.9 %collective-permute-start.1 = (bf16[2,4,512,128]{3,2,1,0:T(8,128)(2,1)}, bf16[2,4,512,128]{3,2,1,0:T(8,128)(2,1)S(1)}, u32[]{:S(2)}, u32[]{:S(2)}) collective-permute-start(bf16[2,4,512,128]{3,2,1,0:T(8,128)(2,1)} %bitcast.96), channel_id=1, source_target_pairs={{0,8},{8,0},{16,24},{1,9},{9,1},{17,25},{2,10},{10,2},{18,26},{3,1... | collective-permute-start | bytes 3145736 | tf_op jit(solution)/shard_map/ppermute | solution.py:369
  24.3 9.8 %collective-permute-start = (bf16[2,4,512,128]{3,2,1,0:T(8,128)(2,1)}, bf16[2,4,512,128]{3,2,1,0:T(8,128)(2,1)S(1)}, u32[]{:S(2)}, u32[]{:S(2)}) collective-permute-start(bf16[2,4,512,128]{3,2,1,0:T(8,128)(2,1)} %bitcast.95), channel_id=1, source_target_pairs={{0,8},{1,9},{2,10},{3,11},{4,12},{5,13},{6,14},{7,15}} | collective-permute-start | bytes 3145736 | tf_op jit(solution)/shard_map/ppermute | solution.py:370
  26.7 7.3 %copy-start = (bf16[8,4,128,128]{3,2,1,0:T(8,128)(2,1)S(1)}, bf16[8,4,128,128]{3,2,1,0:T(8,128)(2,1)}, u32[]{:S(2)}) copy-start(bf16[8,4,128,128]{3,2,1,0:T(8,128)(2,1)} %get-tuple-element.9) | copy-start | bytes 3145732
  28.4 18.3 %collective-permute-start.2 = (bf16[2,4,256,128]{3,2,1,0:T(8,128)(2,1)S(1)}, bf16[2,4,256,128]{3,2,1,0:T(8,128)(2,1)S(1)}, u32[]{:S(2)}, u32[]{:S(2)}) collective-permute-start(bf16[2,4,256,128]{3,2,1,0:T(8,128)(2,1)S(1)} %slice.167), channel_id=1, source_target_pairs={{0,16},{8,24},{1,17},{9,25},{2,18},{10,26},{3,19},{11,27},{4,20},{... | collective-permute-start | bytes 1572872 | tf_op jit(solution)/shard_map/ppermute | solution.py:373
  32.6 9.2 %collective-permute-start.11 = (bf16[4,256,128]{2,1,0:T(8,128)(2,1)S(1)}, bf16[4,256,128]{2,1,0:T(8,128)(2,1)S(1)}, u32[]{:S(2)}, u32[]{:S(2)}) collective-permute-start(bf16[4,256,128]{2,1,0:T(8,128)(2,1)S(1)} %fusion.5), channel_id=1, source_target_pairs={{0,1},{1,0},{2,3},{3,2},{4,5},{5,4},{6,7},{7,6},{8,9},{9,8},{10,11... | collective-permute-start | bytes 786440 | tf_op jit(solution)/shard_map/ppermute | solution.py:357
  34.3 12.2 %collective-permute-start.7 = (bf16[4,256,128]{2,1,0:T(8,128)(2,1)S(1)}, bf16[4,256,128]{2,1,0:T(8,128)(2,1)S(1)}, u32[]{:S(2)}, u32[]{:S(2)}) collective-permute-start(bf16[4,256,128]{2,1,0:T(8,128)(2,1)S(1)} %fusion.4), channel_id=1, source_target_pairs={{0,1},{1,0},{2,3},{3,2},{4,5},{5,4},{6,7},{7,6},{8,9},{9,8},{10,11... | collective-permute-start | bytes 786440 | tf_op jit(solution)/shard_map/ppermute | solution.py:357
  41.9 12.1 %collective-permute-start.12 = (bf16[256,128]{1,0:T(8,128)(2,1)S(1)}, bf16[256,128]{1,0:T(8,128)(2,1)S(1)}, u32[]{:S(2)}, u32[]{:S(2)}) collective-permute-start(bf16[256,128]{1,0:T(8,128)(2,1)S(1)} %get-tuple-element.25), channel_id=1, source_target_pairs={{0,2},{1,3},{2,0},{3,1},{4,6},{5,7},{6,4},{7,5},{8,10},{9,11},{10,... | collective-permute-start | bytes 196616 | tf_op jit(solution)/shard_map/ppermute | solution.py:357
  43.5 12.4 %collective-permute-start.13 = (bf16[256,128]{1,0:T(8,128)(2,1)S(1)}, bf16[256,128]{1,0:T(8,128)(2,1)S(1)}, u32[]{:S(2)}, u32[]{:S(2)}) collective-permute-start(bf16[256,128]{1,0:T(8,128)(2,1)S(1)} %get-tuple-element.27), channel_id=1, source_target_pairs={{0,4},{1,5},{2,6},{3,7},{4,0},{5,1},{6,2},{7,3},{8,12},{9,13},{10,... | collective-permute-start | bytes 196616 | tf_op jit(solution)/shard_map/ppermute | solution.py:357
  46.1 12.4 %collective-permute-start.14 = (bf16[256,128]{1,0:T(8,128)(2,1)S(1)}, bf16[256,128]{1,0:T(8,128)(2,1)S(1)}, u32[]{:S(2)}, u32[]{:S(2)}) collective-permute-start(bf16[256,128]{1,0:T(8,128)(2,1)S(1)} %get-tuple-element.26), channel_id=1, source_target_pairs={{0,6},{1,7},{2,4},{3,5},{4,2},{5,3},{6,0},{7,1},{8,14},{9,15},{10,... | collective-permute-start | bytes 196616 | tf_op jit(solution)/shard_map/ppermute | solution.py:357
  46.8 13.0 %collective-permute-start.3 = (bf16[4,256,128]{2,1,0:T(8,128)(2,1)S(1)}, bf16[4,256,128]{2,1,0:T(8,128)(2,1)S(1)}, u32[]{:S(2)}, u32[]{:S(2)}) collective-permute-start(bf16[4,256,128]{2,1,0:T(8,128)(2,1)S(1)} %fusion.3), channel_id=1, source_target_pairs={{0,1},{1,0},{2,3},{3,2},{4,5},{5,4},{6,7},{7,6},{8,9},{9,8},{10,11... | collective-permute-start | bytes 786440 | tf_op jit(solution)/shard_map/ppermute | solution.py:357
  48.3 13.1 %collective-permute-start.10 = (bf16[256,128]{1,0:T(8,128)(2,1)S(1)}, bf16[256,128]{1,0:T(8,128)(2,1)S(1)}, u32[]{:S(2)}, u32[]{:S(2)}) collective-permute-start(bf16[256,128]{1,0:T(8,128)(2,1)S(1)} %get-tuple-element.23), channel_id=1, source_target_pairs={{0,6},{1,7},{2,4},{3,5},{4,2},{5,3},{6,0},{7,1},{8,14},{9,15},{10,... | collective-permute-start | bytes 196616 | tf_op jit(solution)/shard_map/ppermute | solution.py:357
  54.0 10.3 %collective-permute-start.8 = (bf16[256,128]{1,0:T(8,128)(2,1)S(1)}, bf16[256,128]{1,0:T(8,128)(2,1)S(1)}, u32[]{:S(2)}, u32[]{:S(2)}) collective-permute-start(bf16[256,128]{1,0:T(8,128)(2,1)S(1)} %get-tuple-element.22), channel_id=1, source_target_pairs={{0,2},{1,3},{2,0},{3,1},{4,6},{5,7},{6,4},{7,5},{8,10},{9,11},{10,... | collective-permute-start | bytes 196616 | tf_op jit(solution)/shard_map/ppermute | solution.py:357
  55.9 8.5 %collective-permute-start.9 = (bf16[256,128]{1,0:T(8,128)(2,1)S(1)}, bf16[256,128]{1,0:T(8,128)(2,1)S(1)}, u32[]{:S(2)}, u32[]{:S(2)}) collective-permute-start(bf16[256,128]{1,0:T(8,128)(2,1)S(1)} %get-tuple-element.24), channel_id=1, source_target_pairs={{0,4},{1,5},{2,6},{3,7},{4,0},{5,1},{6,2},{7,3},{8,12},{9,13},{10,... | collective-permute-start | bytes 196616 | tf_op jit(solution)/shard_map/ppermute | solution.py:357
  58.5 5.9 %collective-permute-start.15 = (f32[256,128]{1,0:T(8,128)S(1)}, f32[256,128]{1,0:T(8,128)S(1)}, u32[]{:S(2)}, u32[]{:S(2)}) collective-permute-start(f32[256,128]{1,0:T(8,128)S(1)} %fusion.8), channel_id=1, source_target_pairs={{0,16},{8,24},{1,17},{9,25},{2,18},{10,26},{3,19},{11,27},{4,20},{... | collective-permute-start | bytes 393224 | tf_op jit(solution)/shard_map/ppermute | solution.py:377
  60.0 4.5 %collective-permute-start.4 = (bf16[256,128]{1,0:T(8,128)(2,1)S(1)}, bf16[256,128]{1,0:T(8,128)(2,1)S(1)}, u32[]{:S(2)}, u32[]{:S(2)}) collective-permute-start(bf16[256,128]{1,0:T(8,128)(2,1)S(1)} %get-tuple-element.19), channel_id=1, source_target_pairs={{0,2},{1,3},{2,0},{3,1},{4,6},{5,7},{6,4},{7,5},{8,10},{9,11},{10,... | collective-permute-start | bytes 196616 | tf_op jit(solution)/shard_map/ppermute | solution.py:357
  61.4 6.6 %collective-permute-start.5 = (bf16[256,128]{1,0:T(8,128)(2,1)S(1)}, bf16[256,128]{1,0:T(8,128)(2,1)S(1)}, u32[]{:S(2)}, u32[]{:S(2)}) collective-permute-start(bf16[256,128]{1,0:T(8,128)(2,1)S(1)} %get-tuple-element.21), channel_id=1, source_target_pairs={{0,4},{1,5},{2,6},{3,7},{4,0},{5,1},{6,2},{7,3},{8,12},{9,13},{10,... | collective-permute-start | bytes 196616 | tf_op jit(solution)/shard_map/ppermute | solution.py:357
  64.3 6.1 %collective-permute-start.6 = (bf16[256,128]{1,0:T(8,128)(2,1)S(1)}, bf16[256,128]{1,0:T(8,128)(2,1)S(1)}, u32[]{:S(2)}, u32[]{:S(2)}) collective-permute-start(bf16[256,128]{1,0:T(8,128)(2,1)S(1)} %get-tuple-element.20), channel_id=1, source_target_pairs={{0,6},{1,7},{2,4},{3,5},{4,2},{5,3},{6,0},{7,1},{8,14},{9,15},{10,... | collective-permute-start | bytes 196616 | tf_op jit(solution)/shard_map/ppermute | solution.py:357

commit v3 on v2

--- a/solution.py
+++ b/solution.py
@@ -32,7 +32,6 @@
 def kernel(
     feats,
     relative,
-    pos_ref,
     ids_hbm,
     res_hbm,
     enc_hbm,
@@ -67,7 +66,7 @@
     max_blocks = slots // LANES
     ring = buf.shape[0]
     wides = acc.shape[1]
-    section_pos, feat_pos = pos_ref[0], pos_ref[1]
+    section_pos, feat_pos = lax.axis_index("section"), lax.axis_index("feat")
     core = section_pos % 2
 
     ids_copy = pltpu.make_async_copy(ids_hbm, ids_v, small_sem.at[0])
@@ -285,7 +284,7 @@
                 out_copy(pair, part, wide, 0).wait()
 
 
-def partial_sums(position, ids, residual, enc, dec, feats, relative):
+def partial_sums(ids, residual, enc, dec, feats, relative):
     tokens, width = residual.shape
     shard = enc.shape[1]
     tiles = width // LANES
@@ -298,7 +297,7 @@
     return pl.pallas_call(
         functools.partial(kernel, feats, relative),
         out_shape=[jax.ShapeDtypeStruct((wides, WIDE, tokens, LANES), BF16)] * 4,
-        in_specs=[pl.BlockSpec(memory_space=pltpu.SMEM)] + [pl.BlockSpec(memory_space=pl.ANY)] * 4,
+        in_specs=[pl.BlockSpec(memory_space=pl.ANY)] * 4,
         out_specs=[pl.BlockSpec(memory_space=pl.ANY)] * 4,
         scratch_shapes=[
             pltpu.VMEM(ids.shape, jnp.int32),
@@ -324,7 +323,7 @@
         cost_estimate=pl.CostEstimate(
             flops=4 * tokens * width * shard, bytes_accessed=2 * width * shard * 3, transcendentals=0
         ),
-    )(position, ids, residual, enc, dec)
+    )(ids, residual, enc, dec)
 
 
 def local(residual, enc_weight, dec_weight, latent_ids):
@@ -336,10 +335,9 @@
     tiles = width // LANES
     own = width // feats
     relative = own == WIDE * LANES
-    position = jnp.stack([section_pos, feat_pos]).astype(jnp.int32)
     ids = latent_ids[0].T
     dec = dec_weight[0].reshape(shard, 2, 2, tiles, LANES).transpose(0, 3, 1, 2, 4)
-    sums = partial_sums(position, ids, residual[0], enc_weight[0], dec, feats, relative)
+    sums = partial_sums(ids, residual[0], enc_weight[0], dec, feats, relative)
 
     def blocks_of(part):
         if relative:
@@ -362,7 +360,7 @@
     def finish(x, sections):
         narrow = x.astype(BF16)
         total = x[0]
-        for device in range(1, feats // 2):
+        for device in reversed(range(1, feats // 2)):
             total = total + across_feat(narrow[device], 2 * device, sections).astype(F32)
         return total
 
@@ -371,9 +369,10 @@
     half = own // 2
     is_low = section_pos < 2
     crossed = lax.ppermute(late[:, :, :half].astype(BF16), "section", [(0, 2), (1, 3)]).astype(F32)
-    second_late = finish(halve(late[:, :, half:], everyone), everyone)
+    second = [halve(late[:, :, half:], everyone), halve(early[:, :, half:], low)]
+    second = finish(jnp.concatenate(second, axis=1), everyone)
+    second_late, second_early = second[:half], second[half:]
     first = finish(halve(jnp.where(is_low, early[:, :, :half], late[:, :, :half] + crossed), everyone), everyone)
-    second_early = finish(halve(early[:, :, half:], low), low)
     carried = lax.ppermute(second_late, "section", [(0, 2), (1, 3)])
     written = jnp.concatenate([first, jnp.where(is_low, second_early, second_late + carried)], axis=0)
     if relative:

time: 71.5 us -> 67.5 us (0.944)
  starting transfers between devices: 34.4 us -> 23.5 us
  waiting for transfers between devices: 11.5 us -> 18.4 us
  local copies, waits for them, and re-layouts: 1.01 us -> 2.36 us
    ppermute x12 -> x9, starting transfers between devices: 24.5 us -> 16.4 us  [across_feat(): return lax.ppermute(x, ('section', 'feat'), pairs)]
    ppermute x12 -> x9, waiting for transfers between devices: 11 us -> 17.7 us  [across_feat(): return lax.ppermute(x, ('section', 'feat'), pairs)]
    ppermute x1, starting transfers between devices: 4.16 us -> 1.45 us  [local(): lax.ppermute(late[:, :, :half].astype(BF16), 'section', [(0, 2), (1, 3)])]
    unnamed x2 -> x6, local copies, waits for them, and re-layouts: 0.01 us -> 1.34 us
    pallas_call x1, Pallas kernels: 21.2 us -> 20.5 us  [partial_sums(): pl.pallas_call(functools.partial(kernel, feats, relative), out_shape=[jax...]
  transfers between devices with their start and end apart: 16 -> 13, of which waited for: 5 -> 7; matrix products, arithmetic and copies ran while one was open for 3% -> 4% of each run, Pallas kernels for 0% -> 0%
where the time goes in v3:
time: 67.5 us; the launch traced here: 67.2 us
  starting transfers between devices  23.5 us (35%)
  Pallas kernels  20.5 us (30%)
  waiting for transfers between devices  18.4 us (27%)
  local copies, waits for them, and re-layouts  2.36 us (3%)
  other arithmetic  2.29 us (3%)
    pallas_call x1, Pallas kernels, partial_sums(): pl.pallas_call(functools.partial(kernel, feats, relative), out_shape=[jax...  20.5 us
    ppermute x9, waiting for transfers between devices, across_feat(): return lax.ppermute(x, ('section', 'feat'), pairs)  17.7 us
    ppermute x9, starting transfers between devices, across_feat(): return lax.ppermute(x, ('section', 'feat'), pairs)  16.4 us
    ppermute x1, starting transfers between devices, local(): lax.ppermute(send_late, 'section', [(0, 1), (1, 0), (2, 3)]).astype(F32)  2.31 us
    ppermute x1, starting transfers between devices, local(): lax.ppermute(send_early, 'section', [(0, 1)]).astype(F32)  2.08 us
    add x1, other arithmetic, local(): keep_late.astype(F32)  1.52 us
    ppermute x1, starting transfers between devices, local(): lax.ppermute(late[:, :, :half].astype(BF16), 'section', [(0, 2), (1, 3)])  1.45 us
  transfers between devices with their start and end apart: 13, of which 7 were waited for; matrix products, arithmetic and copies ran while one was open for 4% of the time, Pallas kernels for 0%

profile of v3, /device:TPU:0, one launch (start us, length us, event | category | flops | bytes accessed | tf_op | source)
XLA Modules:
  0.0 67.2 jit_solution(16463593437167645076)
XLA Ops:
  0.0 20.5 %shard_map.46 = (bf16[8,4,128,128]{3,2,1,0:T(8,128)(2,1)}, bf16[8,4,128,128]{3,2,1,0:T(8,128)(2,1)}, bf16[8,4,128,128]{3,2,1,0:T(8,128)(2,1)}, bf16[8,4,128,128]{3,2,1,0:T(8,128)(2,1)}) custom-call(s32[64,128]{1,0:T(8,128)} %bitcast.72, bf16[128,4096]{1,0:T(8,128)(2,1)} %bitcast.68, bf16[4096,2048]{1,0:T(8,128)(2,1)} %bitcast.67, ...), custom_call_target="tpu_custom_call" | custom-call | flops 4294967296 | bytes 50331648 | tf_op jit(solution)/shard_map/pallas_call | solution.py:297
  20.5 2.3 %collective-permute-start.1 = (bf16[2,4,512,128]{3,2,1,0:T(8,128)(2,1)}, bf16[2,4,512,128]{3,2,1,0:T(8,128)(2,1)S(1)}, u32[]{:S(2)}, u32[]{:S(2)}) collective-permute-start(bf16[2,4,512,128]{3,2,1,0:T(8,128)(2,1)} %bitcast.74), channel_id=1, source_target_pairs={{0,8},{8,0},{16,24},{1,9},{9,1},{17,25},{2,10},{10,2},{18,26},{3,1... | collective-permute-start | bytes 3145736 | tf_op jit(solution)/shard_map/ppermute | solution.py:367
  22.8 2.1 %collective-permute-start = (bf16[2,4,512,128]{3,2,1,0:T(8,128)(2,1)}, bf16[2,4,512,128]{3,2,1,0:T(8,128)(2,1)S(1)}, u32[]{:S(2)}, u32[]{:S(2)}) collective-permute-start(bf16[2,4,512,128]{3,2,1,0:T(8,128)(2,1)} %bitcast.73), channel_id=1, source_target_pairs={{0,8},{1,9},{2,10},{3,11},{4,12},{5,13},{6,14},{7,15}} | collective-permute-start | bytes 3145736 | tf_op jit(solution)/shard_map/ppermute | solution.py:368
  24.9 0.4 collective-permute-done.1
  25.3 1.5 %convert_add_fusion = f32[2,4,512,128]{3,2,1,0:T(8,128)S(1)} fusion(bf16[2,4,512,128]{3,2,1,0:T(8,128)(2,1)} %bitcast.70, bf16[2,4,512,128]{3,2,1,0:T(8,128)(2,1)S(1)} %collective-permute-done.1), kind=kLoop, calls=%fused_computation | loop fusion | flops 1572864 | bytes 4194304 | tf_op jit(solution)/shard_map/add | solution.py:367
  26.8 3.1 %collective-permute-start.7 = (bf16[4,256,128]{2,1,0:T(8,128)(2,1)S(1)}, bf16[4,256,128]{2,1,0:T(8,128)(2,1)S(1)}, u32[]{:S(2)}, u32[]{:S(2)}) collective-permute-start(bf16[4,256,128]{2,1,0:T(8,128)(2,1)S(1)} %fusion.5), channel_id=1, source_target_pairs={{0,1},{1,0},{2,3},{3,2},{4,5},{5,4},{6,7},{7,6},{8,9},{9,8},{10,11... | collective-permute-start | bytes 786440 | tf_op jit(solution)/shard_map/ppermute | solution.py:355
  30.0 0.0 collective-permute-done
  30.0 0.2 convert_add_fusion.1
  30.2 1.3 %copy-done = f32[2,4,512,128]{3,2,1,0:T(8,128)} copy-done((f32[2,4,512,128]{3,2,1,0:T(8,128)}, f32[2,4,512,128]{3,2,1,0:T(8,128)S(1)}, u32[]{:S(2)}) %copy-start) | copy-done | bytes 2097176
  31.6 2.3 %collective-permute-start.8 = (bf16[4,256,128]{2,1,0:T(8,128)(2,1)S(1)}, bf16[4,256,128]{2,1,0:T(8,128)(2,1)S(1)}, u32[]{:S(2)}, u32[]{:S(2)}) collective-permute-start(bf16[4,256,128]{2,1,0:T(8,128)(2,1)S(1)} %fusion.6), channel_id=1, source_target_pairs={{0,1},{1,0},{2,3},{3,2},{4,5},{5,4},{6,7},{7,6},{8,9},{9,8},{10,11... | collective-permute-start | bytes 786440 | tf_op jit(solution)/shard_map/ppermute | solution.py:355
  33.9 0.1 slice.155
  34.0 1.5 %collective-permute-start.2 = (bf16[2,4,256,128]{3,2,1,0:T(8,128)(2,1)S(1)}, bf16[2,4,256,128]{3,2,1,0:T(8,128)(2,1)S(1)}, u32[]{:S(2)}, u32[]{:S(2)}) collective-permute-start(bf16[2,4,256,128]{3,2,1,0:T(8,128)(2,1)S(1)} %slice.155), channel_id=1, source_target_pairs={{0,16},{8,24},{1,17},{9,25},{2,18},{10,26},{3,19},{11,27},{4,20},{... | collective-permute-start | bytes 1572872 | tf_op jit(solution)/shard_map/ppermute | solution.py:371
  35.5 1.6 %collective-permute-done.7 = bf16[4,256,128]{2,1,0:T(8,128)(2,1)S(1)} collective-permute-done((bf16[4,256,128]{2,1,0:T(8,128)(2,1)S(1)}, bf16[4,256,128]{2,1,0:T(8,128)(2,1)S(1)}, u32[]{:S(2)}, u32[]{:S(2)}) %collective-permute-start.7) | collective-permute-done | bytes 262176 | tf_op jit(solution)/shard_map/ppermute | solution.py:355
  37.1 5.1 %collective-permute-done.8 = bf16[4,256,128]{2,1,0:T(8,128)(2,1)S(1)} collective-permute-done((bf16[4,256,128]{2,1,0:T(8,128)(2,1)S(1)}, bf16[4,256,128]{2,1,0:T(8,128)(2,1)S(1)}, u32[]{:S(2)}, u32[]{:S(2)}) %collective-permute-start.8) | collective-permute-done | bytes 262176 | tf_op jit(solution)/shard_map/ppermute | solution.py:355
  42.2 0.1 fusion.1
  42.3 0.1 fusion
  42.4 2.9 %collective-permute-start.10 = (bf16[512,128]{1,0:T(8,128)(2,1)S(1)}, bf16[512,128]{1,0:T(8,128)(2,1)S(1)}, u32[]{:S(2)}, u32[]{:S(2)}) collective-permute-start(bf16[512,128]{1,0:T(8,128)(2,1)S(1)} %get-tuple-element.17), channel_id=1, source_target_pairs={{0,4},{1,5},{2,6},{3,7},{4,0},{5,1},{6,2},{7,3},{8,12},{9,13},{10,... | collective-permute-start | bytes 393224 | tf_op jit(solution)/shard_map/ppermute | solution.py:355
  45.2 1.5 %collective-permute-start.11 = (bf16[512,128]{1,0:T(8,128)(2,1)S(1)}, bf16[512,128]{1,0:T(8,128)(2,1)S(1)}, u32[]{:S(2)}, u32[]{:S(2)}) collective-permute-start(bf16[512,128]{1,0:T(8,128)(2,1)S(1)} %get-tuple-element.16), channel_id=1, source_target_pairs={{0,2},{1,3},{2,0},{3,1},{4,6},{5,7},{6,4},{7,5},{8,10},{9,11},{10,... | collective-permute-start | bytes 393224 | tf_op jit(solution)/shard_map/ppermute | solution.py:355
  46.8 0.1 collective-permute-start.9
  46.8 0.3 collective-permute-done.2
  47.1 0.2 slice_select_fusion
  47.4 1.5 %collective-permute-start.3 = (bf16[4,256,128]{2,1,0:T(8,128)(2,1)S(1)}, bf16[4,256,128]{2,1,0:T(8,128)(2,1)S(1)}, u32[]{:S(2)}, u32[]{:S(2)}) collective-permute-start(bf16[4,256,128]{2,1,0:T(8,128)(2,1)S(1)} %fusion.4), channel_id=1, source_target_pairs={{0,1},{1,0},{2,3},{3,2},{4,5},{5,4},{6,7},{7,6},{8,9},{9,8},{10,11... | collective-permute-start | bytes 786440 | tf_op jit(solution)/shard_map/ppermute | solution.py:355
  48.9 6.0 %collective-permute-done.10 = bf16[512,128]{1,0:T(8,128)(2,1)S(1)} collective-permute-done((bf16[512,128]{1,0:T(8,128)(2,1)S(1)}, bf16[512,128]{1,0:T(8,128)(2,1)S(1)}, u32[]{:S(2)}, u32[]{:S(2)}) %collective-permute-start.10) | collective-permute-done | bytes 131104 | tf_op jit(solution)/shard_map/ppermute | solution.py:355
  54.9 0.1 fusion.11
  55.0 1.3 %collective-permute-start.12 = (f32[256,128]{1,0:T(8,128)S(1)}, f32[256,128]{1,0:T(8,128)S(1)}, u32[]{:S(2)}, u32[]{:S(2)}) collective-permute-start(f32[256,128]{1,0:T(8,128)S(1)} %slice.100), channel_id=1, source_target_pairs={{0,16},{8,24},{1,17},{9,25},{2,18},{10,26},{3,19},{11,27},{4,20},{... | collective-permute-start | bytes 393224 | tf_op jit(solution)/shard_map/ppermute | solution.py:376
  56.3 0.1 fusion.17
  56.4 2.8 %collective-permute-start.4 = (bf16[256,128]{1,0:T(8,128)(2,1)S(1)}, bf16[256,128]{1,0:T(8,128)(2,1)S(1)}, u32[]{:S(2)}, u32[]{:S(2)}) collective-permute-start(bf16[256,128]{1,0:T(8,128)(2,1)S(1)} %get-tuple-element.18), channel_id=1, source_target_pairs={{0,6},{1,7},{2,4},{3,5},{4,2},{5,3},{6,0},{7,1},{8,14},{9,15},{10,... | collective-permute-start | bytes 196616 | tf_op jit(solution)/shard_map/ppermute | solution.py:355
  59.2 1.7 %collective-permute-start.5 = (bf16[256,128]{1,0:T(8,128)(2,1)S(1)}, bf16[256,128]{1,0:T(8,128)(2,1)S(1)}, u32[]{:S(2)}, u32[]{:S(2)}) collective-permute-start(bf16[256,128]{1,0:T(8,128)(2,1)S(1)} %get-tuple-element.20), channel_id=1, source_target_pairs={{0,4},{1,5},{2,6},{3,7},{4,0},{5,1},{6,2},{7,3},{8,12},{9,13},{10,... | collective-permute-start | bytes 196616 | tf_op jit(solution)/shard_map/ppermute | solution.py:355
  60.9 0.5 collective-permute-start.6
  61.4 1.2 %collective-permute-done.4 = bf16[256,128]{1,0:T(8,128)(2,1)S(1)} collective-permute-done((bf16[256,128]{1,0:T(8,128)(2,1)S(1)}, bf16[256,128]{1,0:T(8,128)(2,1)S(1)}, u32[]{:S(2)}, u32[]{:S(2)}) %collective-permute-start.4) | collective-permute-done | bytes 65568 | tf_op jit(solution)/shard_map/ppermute | solution.py:355
  62.7 3.7 %collective-permute-done.5 = bf16[256,128]{1,0:T(8,128)(2,1)S(1)} collective-permute-done((bf16[256,128]{1,0:T(8,128)(2,1)S(1)}, bf16[256,128]{1,0:T(8,128)(2,1)S(1)}, u32[]{:S(2)}, u32[]{:S(2)}) %collective-permute-start.5) | collective-permute-done | bytes 65568 | tf_op jit(solution)/shard_map/ppermute | solution.py:355
  66.5 0.8 %copy.5 = bf16[4,128,128]{1,2,0:T(8,128)(2,1)} copy(bf16[4,128,128]{2,1,0:T(8,128)(2,1)S(1)} %bitcast.71) | data formatting | bytes 262144 | tf_op jit(solution)/shard_map/convert_element_type | solution.py:380
  (20 shorter events, 0.3 us)
Async XLA Ops:
  20.5 4.8 %collective-permute-start.1 = (bf16[2,4,512,128]{3,2,1,0:T(8,128)(2,1)}, bf16[2,4,512,128]{3,2,1,0:T(8,128)(2,1)S(1)}, u32[]{:S(2)}, u32[]{:S(2)}) collective-permute-start(bf16[2,4,512,128]{3,2,1,0:T(8,128)(2,1)} %bitcast.74), channel_id=1, source_target_pairs={{0,8},{8,0},{16,24},{1,9},{9,1},{17,25},{2,10},{10,2},{18,26},{3,1... | collective-permute-start | bytes 3145736 | tf_op jit(solution)/shard_map/ppermute | solution.py:367
  22.8 7.2 %collective-permute-start = (bf16[2,4,512,128]{3,2,1,0:T(8,128)(2,1)}, bf16[2,4,512,128]{3,2,1,0:T(8,128)(2,1)S(1)}, u32[]{:S(2)}, u32[]{:S(2)}) collective-permute-start(bf16[2,4,512,128]{3,2,1,0:T(8,128)(2,1)} %bitcast.73), channel_id=1, source_target_pairs={{0,8},{1,9},{2,10},{3,11},{4,12},{5,13},{6,14},{7,15}} | collective-permute-start | bytes 3145736 | tf_op jit(solution)/shard_map/ppermute | solution.py:368
  25.3 4.7 %copy-start.2 = (bf16[8,4,128,128]{3,2,1,0:T(8,128)(2,1)S(1)}, bf16[8,4,128,128]{3,2,1,0:T(8,128)(2,1)}, u32[]{:S(2)}) copy-start(bf16[8,4,128,128]{3,2,1,0:T(8,128)(2,1)} %get-tuple-element.9) | copy-start | bytes 3145732
  26.8 10.2 %collective-permute-start.7 = (bf16[4,256,128]{2,1,0:T(8,128)(2,1)S(1)}, bf16[4,256,128]{2,1,0:T(8,128)(2,1)S(1)}, u32[]{:S(2)}, u32[]{:S(2)}) collective-permute-start(bf16[4,256,128]{2,1,0:T(8,128)(2,1)S(1)} %fusion.5), channel_id=1, source_target_pairs={{0,1},{1,0},{2,3},{3,2},{4,5},{5,4},{6,7},{7,6},{8,9},{9,8},{10,11... | collective-permute-start | bytes 786440 | tf_op jit(solution)/shard_map/ppermute | solution.py:355
  30.2 1.3 %copy-start = (f32[2,4,512,128]{3,2,1,0:T(8,128)}, f32[2,4,512,128]{3,2,1,0:T(8,128)S(1)}, u32[]{:S(2)}) copy-start(f32[2,4,512,128]{3,2,1,0:T(8,128)S(1)} %convert_add_fusion.1) | copy-start | bytes 6291460
  31.6 10.6 %collective-permute-start.8 = (bf16[4,256,128]{2,1,0:T(8,128)(2,1)S(1)}, bf16[4,256,128]{2,1,0:T(8,128)(2,1)S(1)}, u32[]{:S(2)}, u32[]{:S(2)}) collective-permute-start(bf16[4,256,128]{2,1,0:T(8,128)(2,1)S(1)} %fusion.6), channel_id=1, source_target_pairs={{0,1},{1,0},{2,3},{3,2},{4,5},{5,4},{6,7},{7,6},{8,9},{9,8},{10,11... | collective-permute-start | bytes 786440 | tf_op jit(solution)/shard_map/ppermute | solution.py:355
  33.9 8.3 %copy-start.1 = (f32[2,4,512,128]{3,2,1,0:T(8,128)S(1)}, f32[2,4,512,128]{3,2,1,0:T(8,128)}, u32[]{:S(2)}) copy-start(f32[2,4,512,128]{3,2,1,0:T(8,128)} %copy-done) | copy-start | bytes 6291460
  34.0 13.1 %collective-permute-start.2 = (bf16[2,4,256,128]{3,2,1,0:T(8,128)(2,1)S(1)}, bf16[2,4,256,128]{3,2,1,0:T(8,128)(2,1)S(1)}, u32[]{:S(2)}, u32[]{:S(2)}) collective-permute-start(bf16[2,4,256,128]{3,2,1,0:T(8,128)(2,1)S(1)} %slice.155), channel_id=1, source_target_pairs={{0,16},{8,24},{1,17},{9,25},{2,18},{10,26},{3,19},{11,27},{4,20},{... | collective-permute-start | bytes 1572872 | tf_op jit(solution)/shard_map/ppermute | solution.py:371
  42.4 12.5 %collective-permute-start.10 = (bf16[512,128]{1,0:T(8,128)(2,1)S(1)}, bf16[512,128]{1,0:T(8,128)(2,1)S(1)}, u32[]{:S(2)}, u32[]{:S(2)}) collective-permute-start(bf16[512,128]{1,0:T(8,128)(2,1)S(1)} %get-tuple-element.17), channel_id=1, source_target_pairs={{0,4},{1,5},{2,6},{3,7},{4,0},{5,1},{6,2},{7,3},{8,12},{9,13},{10,... | collective-permute-start | bytes 393224 | tf_op jit(solution)/shard_map/ppermute | solution.py:355
  45.2 9.7 %collective-permute-start.11 = (bf16[512,128]{1,0:T(8,128)(2,1)S(1)}, bf16[512,128]{1,0:T(8,128)(2,1)S(1)}, u32[]{:S(2)}, u32[]{:S(2)}) collective-permute-start(bf16[512,128]{1,0:T(8,128)(2,1)S(1)} %get-tuple-element.16), channel_id=1, source_target_pairs={{0,2},{1,3},{2,0},{3,1},{4,6},{5,7},{6,4},{7,5},{8,10},{9,11},{10,... | collective-permute-start | bytes 393224 | tf_op jit(solution)/shard_map/ppermute | solution.py:355
  46.8 8.2 %collective-permute-start.9 = (bf16[512,128]{1,0:T(8,128)(2,1)S(1)}, bf16[512,128]{1,0:T(8,128)(2,1)S(1)}, u32[]{:S(2)}, u32[]{:S(2)}) collective-permute-start(bf16[512,128]{1,0:T(8,128)(2,1)S(1)} %get-tuple-element.15), channel_id=1, source_target_pairs={{0,6},{1,7},{2,4},{3,5},{4,2},{5,3},{6,0},{7,1},{8,14},{9,15},{10,... | collective-permute-start | bytes 393224 | tf_op jit(solution)/shard_map/ppermute | solution.py:355
  47.4 8.9 %collective-permute-start.3 = (bf16[4,256,128]{2,1,0:T(8,128)(2,1)S(1)}, bf16[4,256,128]{2,1,0:T(8,128)(2,1)S(1)}, u32[]{:S(2)}, u32[]{:S(2)}) collective-permute-start(bf16[4,256,128]{2,1,0:T(8,128)(2,1)S(1)} %fusion.4), channel_id=1, source_target_pairs={{0,1},{1,0},{2,3},{3,2},{4,5},{5,4},{6,7},{7,6},{8,9},{9,8},{10,11... | collective-permute-start | bytes 786440 | tf_op jit(solution)/shard_map/ppermute | solution.py:355
  55.0 6.4 %collective-permute-start.12 = (f32[256,128]{1,0:T(8,128)S(1)}, f32[256,128]{1,0:T(8,128)S(1)}, u32[]{:S(2)}, u32[]{:S(2)}) collective-permute-start(f32[256,128]{1,0:T(8,128)S(1)} %slice.100), channel_id=1, source_target_pairs={{0,16},{8,24},{1,17},{9,25},{2,18},{10,26},{3,19},{11,27},{4,20},{... | collective-permute-start | bytes 393224 | tf_op jit(solution)/shard_map/ppermute | solution.py:376
  56.4 6.2 %collective-permute-start.4 = (bf16[256,128]{1,0:T(8,128)(2,1)S(1)}, bf16[256,128]{1,0:T(8,128)(2,1)S(1)}, u32[]{:S(2)}, u32[]{:S(2)}) collective-permute-start(bf16[256,128]{1,0:T(8,128)(2,1)S(1)} %get-tuple-element.18), channel_id=1, source_target_pairs={{0,6},{1,7},{2,4},{3,5},{4,2},{5,3},{6,0},{7,1},{8,14},{9,15},{10,... | collective-permute-start | bytes 196616 | tf_op jit(solution)/shard_map/ppermute | solution.py:355
  59.2 7.2 %collective-permute-start.5 = (bf16[256,128]{1,0:T(8,128)(2,1)S(1)}, bf16[256,128]{1,0:T(8,128)(2,1)S(1)}, u32[]{:S(2)}, u32[]{:S(2)}) collective-permute-start(bf16[256,128]{1,0:T(8,128)(2,1)S(1)} %get-tuple-element.20), channel_id=1, source_target_pairs={{0,4},{1,5},{2,6},{3,7},{4,0},{5,1},{6,2},{7,3},{8,12},{9,13},{10,... | collective-permute-start | bytes 196616 | tf_op jit(solution)/shard_map/ppermute | solution.py:355
  60.9 5.5 %collective-permute-start.6 = (bf16[256,128]{1,0:T(8,128)(2,1)S(1)}, bf16[256,128]{1,0:T(8,128)(2,1)S(1)}, u32[]{:S(2)}, u32[]{:S(2)}) collective-permute-start(bf16[256,128]{1,0:T(8,128)(2,1)S(1)} %get-tuple-element.19), channel_id=1, source_target_pairs={{0,2},{1,3},{2,0},{3,1},{4,6},{5,7},{6,4},{7,5},{8,10},{9,11},{10,... | collective-permute-start | bytes 196616 | tf_op jit(solution)/shard_map/ppermute | solution.py:355

commit v4 on v3

--- a/solution.py
+++ b/solution.py
@@ -368,11 +368,12 @@
     early = keep_early.astype(F32) + lax.ppermute(send_early, "section", [(0, 1)]).astype(F32)
     half = own // 2
     is_low = section_pos < 2
-    crossed = lax.ppermute(late[:, :, :half].astype(BF16), "section", [(0, 2), (1, 3)]).astype(F32)
+    crossing = lax.optimization_barrier(late[:, :, :half].astype(BF16))
+    crossed = lax.ppermute(crossing, "section", [(0, 2), (1, 3)]).astype(F32)
     second = [halve(late[:, :, half:], everyone), halve(early[:, :, half:], low)]
     second = finish(jnp.concatenate(second, axis=1), everyone)
     second_late, second_early = second[:half], second[half:]
-    first = finish(halve(jnp.where(is_low, early[:, :, :half], late[:, :, :half] + crossed), everyone), everyone)
+    first = finish(halve(jnp.where(is_low, early[:, :, :half], crossing.astype(F32) + crossed), everyone), everyone)
     carried = lax.ppermute(second_late, "section", [(0, 2), (1, 3)])
     written = jnp.concatenate([first, jnp.where(is_low, second_early, second_late + carried)], axis=0)
     if relative:

time: 67.5 us -> 72.2 us (1.070)
  waiting for transfers between devices: 18.4 us -> 22.2 us
  other arithmetic: 2.29 us -> 4.82 us
  starting transfers between devices: 23.5 us -> 21.9 us
    ppermute x9, waiting for transfers between devices: 17.7 us -> 21.7 us  [across_feat(): return lax.ppermute(x, ('section', 'feat'), pairs)]
    another operation x2 -> x3, other arithmetic: 0.06 us -> 1.73 us
    add x1 -> x0, other arithmetic: 1.52 us -> none  [local(): keep_late.astype(F32)]
    ppermute x9, starting transfers between devices: 16.4 us -> 15 us  [across_feat(): return lax.ppermute(x, ('section', 'feat'), pairs)]
    convert_element_type x3, local copies, waits for them, and re-layouts: 0.11 us -> 1.52 us  [halve(): return x[0] + across_feat(x[1].astype(BF16), 1, sections).astype(F32)]
    unnamed x6 -> x2, local copies, waits for them, and re-layouts: 1.34 us -> 0.01 us
    add x1, other arithmetic: 0.21 us -> 1.52 us  [local(): keep_early.astype(F32)]
    add x2, other arithmetic: 0.1 us -> 1.2 us  [halve(): return x[0] + across_feat(x[1].astype(BF16), 1, sections).astype(F32)]
  transfers between devices with their start and end apart: 13 -> 13, of which waited for: 7 -> 8; matrix products, arithmetic and copies ran while one was open for 4% -> 9% of each run, Pallas kernels for 0% -> 0%
where the time goes in v4:
time: 72.2 us; the launch traced here: 71.9 us
  waiting for transfers between devices  22.2 us (31%)
  starting transfers between devices  21.9 us (30%)
  Pallas kernels  20.4 us (28%)
  other arithmetic  4.82 us (7%)
  local copies, waits for them, and re-layouts  2.38 us (3%)
    ppermute x9, waiting for transfers between devices, across_feat(): return lax.ppermute(x, ('section', 'feat'), pairs)  21.7 us
    pallas_call x1, Pallas kernels, partial_sums(): pl.pallas_call(functools.partial(kernel, feats, relative), out_shape=[jax...  20.4 us
    ppermute x9, starting transfers between devices, across_feat(): return lax.ppermute(x, ('section', 'feat'), pairs)  15 us
    ppermute x1, starting transfers between devices, local(): lax.ppermute(send_early, 'section', [(0, 1)]).astype(F32)  2.4 us
    ppermute x1, starting transfers between devices, local(): lax.ppermute(send_late, 'section', [(0, 1), (1, 0), (2, 3)]).astype(F32)  1.92 us
    another operation x3, other arithmetic  1.73 us
    convert_element_type x3, local copies, waits for them, and re-layouts, halve(): return x[0] + across_feat(x[1].astype(BF16), 1, sections).astype(F32)  1.52 us
    add x1, other arithmetic, local(): keep_early.astype(F32)  1.52 us
  transfers between devices with their start and end apart: 13, of which 8 were waited for; matrix products, arithmetic and copies ran while one was open for 9% of the time, Pallas kernels for 0%

profile of v4, /device:TPU:0, one launch (start us, length us, event | category | flops | bytes accessed | tf_op | source)
XLA Modules:
  0.0 71.9 jit_solution(14217641354569085992)
XLA Ops:
  0.0 20.4 %shard_map.46 = (bf16[8,4,128,128]{3,2,1,0:T(8,128)(2,1)}, bf16[8,4,128,128]{3,2,1,0:T(8,128)(2,1)}, bf16[8,4,128,128]{3,2,1,0:T(8,128)(2,1)}, bf16[8,4,128,128]{3,2,1,0:T(8,128)(2,1)}) custom-call(s32[64,128]{1,0:T(8,128)} %bitcast.72, bf16[128,4096]{1,0:T(8,128)(2,1)} %bitcast.68, bf16[4096,2048]{1,0:T(8,128)(2,1)} %bitcast.67, ...), custom_call_target="tpu_custom_call" | custom-call | flops 4294967296 | bytes 50331648 | tf_op jit(solution)/shard_map/pallas_call | solution.py:297
  20.4 2.4 %collective-permute-start = (bf16[2,4,512,128]{3,2,1,0:T(8,128)(2,1)}, bf16[2,4,512,128]{3,2,1,0:T(8,128)(2,1)S(1)}, u32[]{:S(2)}, u32[]{:S(2)}) collective-permute-start(bf16[2,4,512,128]{3,2,1,0:T(8,128)(2,1)} %bitcast.74), channel_id=1, source_target_pairs={{0,8},{1,9},{2,10},{3,11},{4,12},{5,13},{6,14},{7,15}} | collective-permute-start | bytes 3145736 | tf_op jit(solution)/shard_map/ppermute | solution.py:368
  22.8 1.9 %collective-permute-start.1 = (bf16[2,4,512,128]{3,2,1,0:T(8,128)(2,1)}, bf16[2,4,512,128]{3,2,1,0:T(8,128)(2,1)S(1)}, u32[]{:S(2)}, u32[]{:S(2)}) collective-permute-start(bf16[2,4,512,128]{3,2,1,0:T(8,128)(2,1)} %bitcast.73), channel_id=1, source_target_pairs={{0,8},{8,0},{16,24},{1,9},{9,1},{17,25},{2,10},{10,2},{18,26},{3,1... | collective-permute-start | bytes 3145736 | tf_op jit(solution)/shard_map/ppermute | solution.py:367
  24.8 0.5 collective-permute-done
  25.2 1.5 %convert_add_fusion.1 = f32[2,4,512,128]{3,2,1,0:T(8,128)S(1)} fusion(bf16[2,4,512,128]{3,2,1,0:T(8,128)(2,1)} %bitcast.70, bf16[2,4,512,128]{3,2,1,0:T(8,128)(2,1)S(1)} %collective-permute-done), kind=kLoop, calls=%fused_computation.1 | loop fusion | flops 1572864 | bytes 4194304 | tf_op jit(solution)/shard_map/add | solution.py:368
  26.8 0.7 %fusion.5 = bf16[4,256,128]{2,1,0:T(8,128)(2,1)} fusion(f32[2,4,512,128]{3,2,1,0:T(8,128)S(1)} %convert_add_fusion.1), kind=kLoop, calls=%fused_computation.16 | loop fusion | bytes 524288 | tf_op jit(solution)/shard_map/convert_element_type | solution.py:358
  27.5 4.2 %collective-permute-start.8 = (bf16[4,256,128]{2,1,0:T(8,128)(2,1)}, bf16[4,256,128]{2,1,0:T(8,128)(2,1)S(1)}, u32[]{:S(2)}, u32[]{:S(2)}) collective-permute-start(bf16[4,256,128]{2,1,0:T(8,128)(2,1)} %fusion.5), channel_id=1, source_target_pairs={{0,1},{1,0},{2,3},{3,2},{4,5},{5,4},{6,7},{7,6},{8,9},{9,8},{10,11... | collective-permute-start | bytes 786440 | tf_op jit(solution)/shard_map/ppermute | solution.py:355
  31.8 0.0 collective-permute-done.1
  31.8 1.7 %fusion.16 = (bf16[2,4,512,128]{3,2,1,0:T(8,128)(2,1)S(1)}, f32[2,4,512,128]{3,2,1,0:T(8,128)}) fusion(bf16[2,4,512,128]{3,2,1,0:T(8,128)(2,1)S(1)} %collective-permute-done.1, bf16[2,4,512,128]{3,2,1,0:T(8,128)(2,1)S(1)} %bitcast.69), kind=kLoop, calls=%fused_computation.37 | loop fusion | flops 2097152 | bytes 5242880 | tf_op jit(solution)/shard_map/convert.7
  33.5 0.7 %slice_bitcast_fusion.3 = bf16[4,256,128]{2,1,0:T(8,128)(2,1)} fusion(bf16[2,4,512,128]{3,2,1,0:T(8,128)(2,1)S(1)} %get-tuple-element.15), kind=kLoop, calls=%fused_computation.22 | loop fusion | bytes 524288 | tf_op jit(solution)/shard_map/convert_element_type | solution.py:358
  34.2 0.0 collective-permute-start.7
  34.2 1.3 %collective-permute-start.2 = (bf16[2,4,256,128]{3,2,1,0:T(8,128)(2,1)S(1)}, bf16[2,4,256,128]{3,2,1,0:T(8,128)(2,1)S(1)}, u32[]{:S(2)}, u32[]{:S(2)}) collective-permute-start(bf16[2,4,256,128]{3,2,1,0:T(8,128)(2,1)S(1)} %slice.83), channel_id=1, source_target_pairs={{0,16},{8,24},{1,17},{9,25},{2,18},{10,26},{3,19},{11,27},{4,20},{... | collective-permute-start | bytes 1572872 | tf_op jit(solution)/shard_map/ppermute | solution.py:372
  35.6 3.5 %collective-permute-done.8 = bf16[4,256,128]{2,1,0:T(8,128)(2,1)S(1)} collective-permute-done((bf16[4,256,128]{2,1,0:T(8,128)(2,1)}, bf16[4,256,128]{2,1,0:T(8,128)(2,1)S(1)}, u32[]{:S(2)}, u32[]{:S(2)}) %collective-permute-start.8) | collective-permute-done | bytes 262176 | tf_op jit(solution)/shard_map/ppermute | solution.py:355
  39.1 5.4 %collective-permute-done.7 = bf16[4,256,128]{2,1,0:T(8,128)(2,1)} collective-permute-done((bf16[4,256,128]{2,1,0:T(8,128)(2,1)}, bf16[4,256,128]{2,1,0:T(8,128)(2,1)}, u32[]{:S(2)}, u32[]{:S(2)}) %collective-permute-start.7) | collective-permute-done | bytes 262176 | tf_op jit(solution)/shard_map/ppermute | solution.py:355
  44.5 1.2 %fusion.2 = f32[4,256,128]{2,1,0:T(8,128)S(1)} fusion(f32[2,4,512,128]{3,2,1,0:T(8,128)} %get-tuple-element.16, bf16[4,256,128]{2,1,0:T(8,128)(2,1)} %collective-permute-done.7), kind=kLoop, calls=%fused_computation.11 | loop fusion | flops 262144 | bytes 1310720 | tf_op jit(solution)/shard_map/add | solution.py:358
  45.7 0.1 fusion
  45.8 2.0 %collective-permute-start.11 = (bf16[512,128]{1,0:T(8,128)(2,1)S(1)}, bf16[512,128]{1,0:T(8,128)(2,1)S(1)}, u32[]{:S(2)}, u32[]{:S(2)}) collective-permute-start(bf16[512,128]{1,0:T(8,128)(2,1)S(1)} %get-tuple-element.18), channel_id=1, source_target_pairs={{0,2},{1,3},{2,0},{3,1},{4,6},{5,7},{6,4},{7,5},{8,10},{9,11},{10,... | collective-permute-start | bytes 393224 | tf_op jit(solution)/shard_map/ppermute | solution.py:355
  47.8 2.5 %collective-permute-start.10 = (bf16[512,128]{1,0:T(8,128)(2,1)S(1)}, bf16[512,128]{1,0:T(8,128)(2,1)S(1)}, u32[]{:S(2)}, u32[]{:S(2)}) collective-permute-start(bf16[512,128]{1,0:T(8,128)(2,1)S(1)} %get-tuple-element.19), channel_id=1, source_target_pairs={{0,4},{1,5},{2,6},{3,7},{4,0},{5,1},{6,2},{7,3},{8,12},{9,13},{10,... | collective-permute-start | bytes 393224 | tf_op jit(solution)/shard_map/ppermute | solution.py:355
  50.3 0.1 slice_select_fusion
  50.5 1.8 %collective-permute-start.3 = (bf16[4,256,128]{2,1,0:T(8,128)(2,1)S(1)}, bf16[4,256,128]{2,1,0:T(8,128)(2,1)S(1)}, u32[]{:S(2)}, u32[]{:S(2)}) collective-permute-start(bf16[4,256,128]{2,1,0:T(8,128)(2,1)S(1)} %fusion.4), channel_id=1, source_target_pairs={{0,1},{1,0},{2,3},{3,2},{4,5},{5,4},{6,7},{7,6},{8,9},{9,8},{10,11... | collective-permute-start | bytes 786440 | tf_op jit(solution)/shard_map/ppermute | solution.py:355
  52.2 0.3 collective-permute-done.11
  52.5 7.9 %collective-permute-done.10 = bf16[512,128]{1,0:T(8,128)(2,1)S(1)} collective-permute-done((bf16[512,128]{1,0:T(8,128)(2,1)S(1)}, bf16[512,128]{1,0:T(8,128)(2,1)S(1)}, u32[]{:S(2)}, u32[]{:S(2)}) %collective-permute-start.10) | collective-permute-done | bytes 131104 | tf_op jit(solution)/shard_map/ppermute | solution.py:355
  60.4 0.1 fusion.10
  60.5 1.3 %collective-permute-start.12 = (f32[256,128]{1,0:T(8,128)S(1)}, f32[256,128]{1,0:T(8,128)S(1)}, u32[]{:S(2)}, u32[]{:S(2)}) collective-permute-start(f32[256,128]{1,0:T(8,128)S(1)} %slice.100), channel_id=1, source_target_pairs={{0,16},{8,24},{1,17},{9,25},{2,18},{10,26},{3,19},{11,27},{4,20},{... | collective-permute-start | bytes 393224 | tf_op jit(solution)/shard_map/ppermute | solution.py:377
  61.8 0.1 fusion.17
  61.9 2.0 %collective-permute-start.6 = (bf16[256,128]{1,0:T(8,128)(2,1)S(1)}, bf16[256,128]{1,0:T(8,128)(2,1)S(1)}, u32[]{:S(2)}, u32[]{:S(2)}) collective-permute-start(bf16[256,128]{1,0:T(8,128)(2,1)S(1)} %get-tuple-element.21), channel_id=1, source_target_pairs={{0,2},{1,3},{2,0},{3,1},{4,6},{5,7},{6,4},{7,5},{8,10},{9,11},{10,... | collective-permute-start | bytes 196616 | tf_op jit(solution)/shard_map/ppermute | solution.py:355
  63.9 1.0 %collective-permute-start.5 = (bf16[256,128]{1,0:T(8,128)(2,1)S(1)}, bf16[256,128]{1,0:T(8,128)(2,1)S(1)}, u32[]{:S(2)}, u32[]{:S(2)}) collective-permute-start(bf16[256,128]{1,0:T(8,128)(2,1)S(1)} %get-tuple-element.22), channel_id=1, source_target_pairs={{0,4},{1,5},{2,6},{3,7},{4,0},{5,1},{6,2},{7,3},{8,12},{9,13},{10,... | collective-permute-start | bytes 196616 | tf_op jit(solution)/shard_map/ppermute | solution.py:355
  64.9 1.4 %collective-permute-start.4 = (bf16[256,128]{1,0:T(8,128)(2,1)S(1)}, bf16[256,128]{1,0:T(8,128)(2,1)S(1)}, u32[]{:S(2)}, u32[]{:S(2)}) collective-permute-start(bf16[256,128]{1,0:T(8,128)(2,1)S(1)} %get-tuple-element.20), channel_id=1, source_target_pairs={{0,6},{1,7},{2,4},{3,5},{4,2},{5,3},{6,0},{7,1},{8,14},{9,15},{10,... | collective-permute-start | bytes 196616 | tf_op jit(solution)/shard_map/ppermute | solution.py:355
  66.4 0.5 collective-permute-done.6
  66.9 3.2 %collective-permute-done.5 = bf16[256,128]{1,0:T(8,128)(2,1)S(1)} collective-permute-done((bf16[256,128]{1,0:T(8,128)(2,1)S(1)}, bf16[256,128]{1,0:T(8,128)(2,1)S(1)}, u32[]{:S(2)}, u32[]{:S(2)}) %collective-permute-start.5) | collective-permute-done | bytes 65568 | tf_op jit(solution)/shard_map/ppermute | solution.py:355
  70.2 0.9 %collective-permute-done.4 = bf16[256,128]{1,0:T(8,128)(2,1)S(1)} collective-permute-done((bf16[256,128]{1,0:T(8,128)(2,1)S(1)}, bf16[256,128]{1,0:T(8,128)(2,1)S(1)}, u32[]{:S(2)}, u32[]{:S(2)}) %collective-permute-start.4) | collective-permute-done | bytes 65568 | tf_op jit(solution)/shard_map/ppermute | solution.py:355
  71.1 0.8 %copy.5 = bf16[4,128,128]{1,2,0:T(8,128)(2,1)} copy(bf16[4,128,128]{2,1,0:T(8,128)(2,1)S(1)} %bitcast.71) | data formatting | bytes 262144 | tf_op jit(solution)/shard_map/convert_element_type | solution.py:381
  (16 shorter events, 0.3 us)
Async XLA Ops:
  20.4 4.8 %collective-permute-start = (bf16[2,4,512,128]{3,2,1,0:T(8,128)(2,1)}, bf16[2,4,512,128]{3,2,1,0:T(8,128)(2,1)S(1)}, u32[]{:S(2)}, u32[]{:S(2)}) collective-permute-start(bf16[2,4,512,128]{3,2,1,0:T(8,128)(2,1)} %bitcast.74), channel_id=1, source_target_pairs={{0,8},{1,9},{2,10},{3,11},{4,12},{5,13},{6,14},{7,15}} | collective-permute-start | bytes 3145736 | tf_op jit(solution)/shard_map/ppermute | solution.py:368
  22.8 8.9 %collective-permute-start.1 = (bf16[2,4,512,128]{3,2,1,0:T(8,128)(2,1)}, bf16[2,4,512,128]{3,2,1,0:T(8,128)(2,1)S(1)}, u32[]{:S(2)}, u32[]{:S(2)}) collective-permute-start(bf16[2,4,512,128]{3,2,1,0:T(8,128)(2,1)} %bitcast.73), channel_id=1, source_target_pairs={{0,8},{8,0},{16,24},{1,9},{9,1},{17,25},{2,10},{10,2},{18,26},{3,1... | collective-permute-start | bytes 3145736 | tf_op jit(solution)/shard_map/ppermute | solution.py:367
  25.2 6.5 %copy-start = (bf16[8,4,128,128]{3,2,1,0:T(8,128)(2,1)S(1)}, bf16[8,4,128,128]{3,2,1,0:T(8,128)(2,1)}, u32[]{:S(2)}) copy-start(bf16[8,4,128,128]{3,2,1,0:T(8,128)(2,1)} %get-tuple-element.11) | copy-start | bytes 3145732
  27.5 11.6 %collective-permute-start.8 = (bf16[4,256,128]{2,1,0:T(8,128)(2,1)}, bf16[4,256,128]{2,1,0:T(8,128)(2,1)S(1)}, u32[]{:S(2)}, u32[]{:S(2)}) collective-permute-start(bf16[4,256,128]{2,1,0:T(8,128)(2,1)} %fusion.5), channel_id=1, source_target_pairs={{0,1},{1,0},{2,3},{3,2},{4,5},{5,4},{6,7},{7,6},{8,9},{9,8},{10,11... | collective-permute-start | bytes 786440 | tf_op jit(solution)/shard_map/ppermute | solution.py:355
  34.2 10.3 %collective-permute-start.7 = (bf16[4,256,128]{2,1,0:T(8,128)(2,1)}, bf16[4,256,128]{2,1,0:T(8,128)(2,1)}, u32[]{:S(2)}, u32[]{:S(2)}) collective-permute-start(bf16[4,256,128]{2,1,0:T(8,128)(2,1)} %slice_bitcast_fusion.3), channel_id=1, source_target_pairs={{0,1},{1,0},{2,3},{3,2},{4,5},{5,4},{6,7},{7,6},{8,9},{9,8},{10,11... | collective-permute-start | bytes 786440 | tf_op jit(solution)/shard_map/ppermute | solution.py:355
  34.2 16.0 %collective-permute-start.2 = (bf16[2,4,256,128]{3,2,1,0:T(8,128)(2,1)S(1)}, bf16[2,4,256,128]{3,2,1,0:T(8,128)(2,1)S(1)}, u32[]{:S(2)}, u32[]{:S(2)}) collective-permute-start(bf16[2,4,256,128]{3,2,1,0:T(8,128)(2,1)S(1)} %slice.83), channel_id=1, source_target_pairs={{0,16},{8,24},{1,17},{9,25},{2,18},{10,26},{3,19},{11,27},{4,20},{... | collective-permute-start | bytes 1572872 | tf_op jit(solution)/shard_map/ppermute | solution.py:372
  45.8 6.7 %collective-permute-start.11 = (bf16[512,128]{1,0:T(8,128)(2,1)S(1)}, bf16[512,128]{1,0:T(8,128)(2,1)S(1)}, u32[]{:S(2)}, u32[]{:S(2)}) collective-permute-start(bf16[512,128]{1,0:T(8,128)(2,1)S(1)} %get-tuple-element.18), channel_id=1, source_target_pairs={{0,2},{1,3},{2,0},{3,1},{4,6},{5,7},{6,4},{7,5},{8,10},{9,11},{10,... | collective-permute-start | bytes 393224 | tf_op jit(solution)/shard_map/ppermute | solution.py:355
  47.8 12.6 %collective-permute-start.10 = (bf16[512,128]{1,0:T(8,128)(2,1)S(1)}, bf16[512,128]{1,0:T(8,128)(2,1)S(1)}, u32[]{:S(2)}, u32[]{:S(2)}) collective-permute-start(bf16[512,128]{1,0:T(8,128)(2,1)S(1)} %get-tuple-element.19), channel_id=1, source_target_pairs={{0,4},{1,5},{2,6},{3,7},{4,0},{5,1},{6,2},{7,3},{8,12},{9,13},{10,... | collective-permute-start | bytes 393224 | tf_op jit(solution)/shard_map/ppermute | solution.py:355
  50.2 10.1 %collective-permute-start.9 = (bf16[512,128]{1,0:T(8,128)(2,1)S(1)}, bf16[512,128]{1,0:T(8,128)(2,1)S(1)}, u32[]{:S(2)}, u32[]{:S(2)}) collective-permute-start(bf16[512,128]{1,0:T(8,128)(2,1)S(1)} %get-tuple-element.17), channel_id=1, source_target_pairs={{0,6},{1,7},{2,4},{3,5},{4,2},{5,3},{6,0},{7,1},{8,14},{9,15},{10,... | collective-permute-start | bytes 393224 | tf_op jit(solution)/shard_map/ppermute | solution.py:355
  50.5 11.3 %collective-permute-start.3 = (bf16[4,256,128]{2,1,0:T(8,128)(2,1)S(1)}, bf16[4,256,128]{2,1,0:T(8,128)(2,1)S(1)}, u32[]{:S(2)}, u32[]{:S(2)}) collective-permute-start(bf16[4,256,128]{2,1,0:T(8,128)(2,1)S(1)} %fusion.4), channel_id=1, source_target_pairs={{0,1},{1,0},{2,3},{3,2},{4,5},{5,4},{6,7},{7,6},{8,9},{9,8},{10,11... | collective-permute-start | bytes 786440 | tf_op jit(solution)/shard_map/ppermute | solution.py:355
  60.5 5.9 %collective-permute-start.12 = (f32[256,128]{1,0:T(8,128)S(1)}, f32[256,128]{1,0:T(8,128)S(1)}, u32[]{:S(2)}, u32[]{:S(2)}) collective-permute-start(f32[256,128]{1,0:T(8,128)S(1)} %slice.100), channel_id=1, source_target_pairs={{0,16},{8,24},{1,17},{9,25},{2,18},{10,26},{3,19},{11,27},{4,20},{... | collective-permute-start | bytes 393224 | tf_op jit(solution)/shard_map/ppermute | solution.py:377
  61.9 5.0 %collective-permute-start.6 = (bf16[256,128]{1,0:T(8,128)(2,1)S(1)}, bf16[256,128]{1,0:T(8,128)(2,1)S(1)}, u32[]{:S(2)}, u32[]{:S(2)}) collective-permute-start(bf16[256,128]{1,0:T(8,128)(2,1)S(1)} %get-tuple-element.21), channel_id=1, source_target_pairs={{0,2},{1,3},{2,0},{3,1},{4,6},{5,7},{6,4},{7,5},{8,10},{9,11},{10,... | collective-permute-start | bytes 196616 | tf_op jit(solution)/shard_map/ppermute | solution.py:355
  63.9 6.2 %collective-permute-start.5 = (bf16[256,128]{1,0:T(8,128)(2,1)S(1)}, bf16[256,128]{1,0:T(8,128)(2,1)S(1)}, u32[]{:S(2)}, u32[]{:S(2)}) collective-permute-start(bf16[256,128]{1,0:T(8,128)(2,1)S(1)} %get-tuple-element.22), channel_id=1, source_target_pairs={{0,4},{1,5},{2,6},{3,7},{4,0},{5,1},{6,2},{7,3},{8,12},{9,13},{10,... | collective-permute-start | bytes 196616 | tf_op jit(solution)/shard_map/ppermute | solution.py:355
  64.9 6.1 %collective-permute-start.4 = (bf16[256,128]{1,0:T(8,128)(2,1)S(1)}, bf16[256,128]{1,0:T(8,128)(2,1)S(1)}, u32[]{:S(2)}, u32[]{:S(2)}) collective-permute-start(bf16[256,128]{1,0:T(8,128)(2,1)S(1)} %get-tuple-element.20), channel_id=1, source_target_pairs={{0,6},{1,7},{2,4},{3,5},{4,2},{5,3},{6,0},{7,1},{8,14},{9,15},{10,... | collective-permute-start | bytes 196616 | tf_op jit(solution)/shard_map/ppermute | solution.py:355
